TPU v7x, 768 devices: a whole 4x8x12 slice. The times are simulated.
768 devices in a mesh: ctx: 48 (over z, x), exp: 16 (over y, core).
Axes of the slice: x: 4, y: 8, z: 12, core: 2. Of those that a mesh axis runs over, the one named last changes fastest.
Arguments:
- residual_in: bfloat16 [3072, 4096], P('ctx'), may hold values from -12 to 12
- queries: bfloat16 [3072, 8192], P('ctx', 'exp'), may hold values from -40 to 40
- projected_key_value: bfloat16 [2, 3072, 512], P(None, 'ctx'), may hold values from -40 to 40
- query_gain: float32 [128], replicated, may hold values from 0.5 to 7
- key_norm_gain: float32 [128], replicated, may hold values from 0.5 to 7
- output_weight: bfloat16 [8192, 4096], P('exp'), may hold values from -0.0625 to 0.0625
- norm_gain: float32 [4096], replicated, may hold values from 0.5 to 1.5
- gate_weight: bfloat16 [768, 4096, 128], P(('exp', 'ctx')), may hold values from -0.09375 to 0.09375
- up_weight: bfloat16 [768, 4096, 128], P(('exp', 'ctx')), may hold values from -0.09375 to 0.09375
- down_weight: bfloat16 [768, 128, 4096], P(('exp', 'ctx')), may hold values from -0.21875 to 0.21875
- expert_index: int32 [3072, 8], P('ctx'), may hold values from 0 to 127, as said below
- expert_slot: int32 [3072, 8], P('ctx'), may hold values from 0 to 7, as said below
- route_weight: float32 [3072, 8], P('ctx'), may hold values from 0.2 to 1
Outputs:
- layer_out: bfloat16 [3072, 4096], P(('ctx', 'exp'))
Inputs may be any that keep to these rules, and one draw needn't show every extreme that they name: `expert_index`: A token's 8 experts are different; its k-th entry lies in the k-th of 8 equal ranges of expert numbers. `expert_slot`: within each block of 64 consecutive tokens, the choices that name one expert hold slots 0, 1, 2, ... in token order; in every block some expert is named by exactly 8 tokens.
All inputs are finite; a program needn't handle non-finite values.
Results may differ from a plain program's by a relative error of at most 0.024.
The roundings to bfloat16 on the way count: a program that leaves them out, or rounds other values in their place, can miss the bound.
Values may be sent and summed in bfloat16 or wider, within the bound.
No kernel may reach another device: no remote copies, remote signals or barrier semaphores. Data moves between devices by JAX's collectives and lax.ppermute only.
A program may use at most 64 MiB of HBM per device.

v0:
```python
import jax
import jax.numpy as jnp
from jax import lax
from jax.sharding import PartitionSpec as P

QUERY_HEADS = 64
KEY_VALUE_HEADS = 4
EXPERTS = 128
SLICES = 6
CAP = 8


THETA = 1000000.0


def apply_norm(value_rows, gain):
    mean_square = jnp.mean(value_rows * value_rows, axis=-1, keepdims=True)
    return value_rows * lax.rsqrt(mean_square + 1e-06) * gain


def apply_rotation(value_rows, token_positions):
    half = value_rows.shape[-1] // 2
    inverse = THETA ** (-(jnp.arange(half, dtype=jnp.float32) * 2.0 / value_rows.shape[-1]))
    angle = token_positions.astype(jnp.float32)[:, None] * inverse[None, :]
    cosine = jnp.cos(angle)[:, None, :]
    sine = jnp.sin(angle)[:, None, :]
    first = value_rows[..., :half]
    second = value_rows[..., half:]
    return jnp.concatenate(
        [first * cosine - second * sine, second * cosine + first * sine], axis=-1
    )


def body(
    residual_in,
    queries,
    projected_key_value,
    query_gain,
    key_norm_gain,
    output_weight,
    norm_gain,
    gate_weight,
    up_weight,
    down_weight,
    expert_index,
    expert_slot,
    route_weight,
):
    rows = queries.shape[0]
    head_dim = query_gain.shape[0]
    local_heads = queries.shape[1] // head_dim
    ctx_index = lax.axis_index("ctx")
    expert_choice_index = lax.axis_index("exp")
    n_exp = lax.axis_size("exp")
    n_ctx = lax.axis_size("ctx")
    token_positions = ctx_index * rows + jnp.arange(rows, dtype=jnp.int32)
    query_rot = apply_rotation(
        apply_norm(queries.reshape(rows, local_heads, head_dim).astype(jnp.float32), query_gain),
        token_positions,
    ).astype(jnp.bfloat16)
    key_value_head = expert_choice_index * local_heads // (QUERY_HEADS // KEY_VALUE_HEADS)
    kv_block = lax.dynamic_slice_in_dim(projected_key_value, key_value_head * head_dim, head_dim, 2)
    rotated_keys = apply_rotation(
        apply_norm(kv_block[0].astype(jnp.float32)[:, None, :], key_norm_gain), token_positions
    )[:, 0, :].astype(jnp.bfloat16)
    paired = jnp.stack([rotated_keys, kv_block[1]])
    scale = 1.0 / head_dim**0.5
    piece = lax.all_gather(paired, "ctx", axis=1, tiled=True)
    peak = jnp.full((local_heads, rows), -1e30, jnp.float32)
    count = piece.shape[1]
    scores = (
        jnp.einsum("qhd,kd->hqk", query_rot, piece[0], preferred_element_type=jnp.float32) * scale
    )
    key_pos = jnp.arange(count, dtype=jnp.int32)
    visible = (key_pos[None, :] <= token_positions[:, None])[None, :, :]
    block_peak = jnp.max(jnp.where(visible, scores, -1e30), axis=-1)
    new_peak = jnp.maximum(peak, block_peak)
    weights = jnp.where(visible, jnp.exp(scores - new_peak[..., None]), 0.0)
    total = jnp.sum(weights, axis=-1)
    accum = jnp.einsum(
        "hqk,kd->hqd", weights.astype(jnp.bfloat16), piece[1], preferred_element_type=jnp.float32
    )
    peak, total, accum = (new_peak, total, accum)
    attended = (
        jnp.transpose(accum / total[..., None], (1, 0, 2))
        .astype(jnp.bfloat16)
        .reshape(rows, local_heads * head_dim)
    )
    partial_value = jnp.dot(attended, output_weight, preferred_element_type=jnp.float32)
    share = rows // n_exp
    summed = lax.psum(partial_value, "exp")
    stream = residual_in.astype(jnp.float32) + summed
    normed = apply_norm(stream, norm_gain).astype(jnp.bfloat16)
    own_stream = lax.dynamic_slice_in_dim(stream, expert_choice_index * share, share, 0)
    local = EXPERTS // n_exp
    lanes = local * CAP
    local_expert = expert_index - expert_choice_index * local
    owned = (local_expert >= 0) & (local_expert < local)
    target = jnp.where(owned, local_expert * CAP + expert_slot, -1)
    match = target[:, :, None] == jnp.arange(lanes, dtype=jnp.int32)[None, None, :]
    select = jnp.any(match, axis=1).astype(jnp.bfloat16)
    packed = lax.dot_general(
        select, normed, (((0,), (0,)), ((), ())), preferred_element_type=jnp.float32
    ).astype(jnp.bfloat16)
    combine_weights = jnp.sum(jnp.where(match, route_weight[:, :, None], 0.0), axis=1)
    units = gate_weight.shape[0]
    outgoing = jnp.repeat(packed.reshape(local, CAP, -1), SLICES, axis=0).reshape(
        n_ctx, units, CAP, -1
    )
    arrived = lax.all_to_all(outgoing, "ctx", split_axis=0, concat_axis=0, tiled=True)
    gate = jnp.einsum("cund,udf->cunf", arrived, gate_weight, preferred_element_type=jnp.float32)
    upper = jnp.einsum("cund,udf->cunf", arrived, up_weight, preferred_element_type=jnp.float32)
    act = (jax.nn.silu(gate) * upper).astype(jnp.bfloat16)
    pieces = jnp.einsum(
        "cunf,ufd->cund", act, down_weight, preferred_element_type=jnp.float32
    ).astype(jnp.bfloat16)
    returned = lax.all_to_all(pieces, "ctx", split_axis=0, concat_axis=0, tiled=True)
    expert_out = jnp.sum(
        returned.reshape(local, SLICES, CAP, -1).astype(jnp.float32), axis=1
    ).reshape(lanes, -1)
    weights = combine_weights
    mixture = lax.psum_scatter(
        jnp.dot(
            weights, expert_out, precision=lax.Precision.HIGHEST, preferred_element_type=jnp.float32
        ),
        "exp",
        scatter_dimension=0,
        tiled=True,
    )
    return (own_stream + mixture).astype(jnp.bfloat16)


def solution(mesh):
    in_specs = (
        P("ctx", None),
        P("ctx", "exp"),
        P(None, "ctx", None),
        P(),
        P(),
        P("exp", None),
        P(),
        P(("exp", "ctx"), None, None),
        P(("exp", "ctx"), None, None),
        P(("exp", "ctx"), None, None),
        P("ctx", None),
        P("ctx", None),
        P("ctx", None),
    )
    out_specs = P(("ctx", "exp"), None)
    return jax.shard_map(body, mesh=mesh, in_specs=in_specs, out_specs=out_specs, check_vma=False)
```

profile of v0, /device:TPU:1, one launch (start us, length us, event | category | flops | bytes accessed | tf_op | source)
XLA Modules:
  0.0 638.6 jit_solution(554575065382022218)
XLA Ops:
  6.6 0.9 fusion.71
  7.5 0.7 constant_dynamic-slice_fusion
  8.2 0.8 fusion.72
  10.0 0.9 reshape.284
  11.4 1.0 fusion.58
  12.6 115.7 %all-gather.2.cloned.1.call-done = bf16[2,3072,128]{2,1,0:T(8,128)(2,1)} async-done(((bf16[2,64,128]{2,1,0:T(8,128)(2,1)}), bf16[2,3072,128]{2,1,0:T(8,128)(2,1)}) %all-gather.2.cloned.1.call-update) | async-done | bytes 1572880 | tf_op jit(solution)/shard_map/all_gather | solution.py:68
  128.3 1.9 select_reduce_fusion
  130.2 0.8 fusion.7
  131.6 0.8 fusion.38
  132.4 0.9 copy-done.2
  133.3 1.9 fusion.60
  135.5 124.9 %all-reduce.4.cloned.1.call-done = f32[64,4096]{1,0:T(8,128)} async-done(((f32[64,4096]{1,0:T(8,128)}), f32[64,4096]{1,0:T(8,128)}) %all-reduce.4.cloned.1.call-update) | async-done | bytes 1048592 | tf_op jit(solution)/shard_map/psum | solution.py:91
  260.4 1.5 multiply_reduce_fusion
  262.6 119.2 %all_to_all.10 = bf16[48,1,8,4096]{3,2,1,0:T(8,128)(2,1)S(1)} all-to-all(bf16[48,1,8,4096]{3,2,1,0:T(8,128)(2,1)S(1)} %bitcast.119), channel_id=1, replica_groups=mesh['ctx'=48,'exp'=16] {'ctx'}, dimensions={0} | all-to-all | bytes 6291456 | tf_op jit(solution)/shard_map/all_to_all | solution.py:110
  381.8 1.7 copy-done.1
  383.5 1.0 fusion.14
  384.7 7.0 %fusion = bf16[48,1,8,4096]{3,2,1,0:T(8,128)(2,1)} fusion(bf16[1,128,4096]{2,1,0:T(8,128)(2,1)S(1)} %copy-done, bf16[48,1,8,4096]{3,2,1,0:T(8,128)(2,1)} %copy-done.1, bf16[1,4096,128]{2,1,0:T(8,128)(2,1)S(1)} %copy-done.4, f32[48,1,8,128]{3,2,0,1:T(8,128)S(1)} %fusion.14), kind=kOutput, calls=%fused_computation.2 | convolution fusion | flops 807174144 | bytes 8585216 | tf_op jit(solution)/shard_map/cunf,ufd->cund/dot_general | solution.py:114
  391.7 8.4 %all-to-all-start.1 = ((bf16[48,1,8,4096]{3,2,1,0:T(8,128)(2,1)}), bf16[48,1,8,4096]{3,2,1,0:T(8,128)(2,1)}, u32[]{:S(2)}, u32[]{:S(2)}) async-start(bf16[48,1,8,4096]{3,2,1,0:T(8,128)(2,1)} %fusion), calls=%async_computation.1 | async-start | bytes 6291456 | tf_op jit(solution)/shard_map/all_to_all | solution.py:117
  400.5 101.5 %all-to-all-done.1 = bf16[48,1,8,4096]{3,2,1,0:T(8,128)(2,1)} async-done(((bf16[48,1,8,4096]{3,2,1,0:T(8,128)(2,1)}), bf16[48,1,8,4096]{3,2,1,0:T(8,128)(2,1)}, u32[]{:S(2)}, u32[]{:S(2)}) %all-to-all-start.1) | async-done | bytes 3145760 | tf_op jit(solution)/shard_map/all_to_all | solution.py:117
  502.0 2.5 convert_reduce_fusion
  504.5 2.0 fusion.41
  506.6 1.3 dynamic-slice
  508.5 121.9 %all-reduce.6.cloned.1.call-done = f32[64,4096]{1,0:T(8,128)} async-done(((f32[64,4096]{1,0:T(8,128)}), f32[64,4096]{1,0:T(8,128)}) %all-reduce.6.cloned.1.call-update) | async-done | bytes 1048592
  630.5 1.5 fusion.66
  (48 shorter events, 3.9 us)
Async XLA Ops:
  6.5 378.0 %copy-start = (bf16[1,128,4096]{2,1,0:T(8,128)(2,1)S(1)}, bf16[1,128,4096]{2,1,0:T(8,128)(2,1)}, u32[]{:S(2)}) copy-start(bf16[1,128,4096]{2,1,0:T(8,128)(2,1)} %param.22) | copy-start | bytes 3145732
  6.5 121.7 %all-gather.2.cloned.1.call-start = ((), (), s32[]{:S(2)}) async-start(), calls=%async_computation.2 | async-start | bytes 1605632 | tf_op jit(solution)/shard_map/all_gather | solution.py:68
  10.0 250.4 %all-reduce.4.cloned.1.call-start = ((), (), s32[]{:S(2)}) async-start(), calls=%async_computation.3 | async-start | bytes 2097152 | tf_op jit(solution)/shard_map/psum | solution.py:91
  130.2 1.4 copy-start.10
  131.0 2.3 copy-start.2
  133.3 1.9 copy-start.7
  133.3 2.0 copy-start.8
  133.3 127.1 %copy-start.5 = (bf16[64,4096]{1,0:T(8,128)(2,1)S(1)}, bf16[64,4096]{1,0:T(8,128)(2,1)}, u32[]{:S(2)}) copy-start(bf16[64,4096]{1,0:T(8,128)(2,1)} %param.13) | copy-start | bytes 1572868
  135.2 126.7 %copy-start.6 = (f32[4096]{0:T(1024)S(1)}, f32[4096]{0:T(1024)}, u32[]{:S(2)}) copy-start(f32[4096]{0:T(1024)} %param.19) | copy-start | bytes 49156
  262.6 120.9 %copy-start.3 = (bf16[1,4096,128]{2,1,0:T(8,128)(2,1)S(1)}, bf16[1,4096,128]{2,1,0:T(8,128)(2,1)}, u32[]{:S(2)}) copy-start(bf16[1,4096,128]{2,1,0:T(8,128)(2,1)} %param.20) | copy-start | bytes 3145732
  381.8 1.7 copy-start.1
  383.5 1.2 copy-start.4
  391.7 8.5 %copy-start.9 = (f32[64,8]{0,1:T(8,128)S(1)}, f32[64,8]{0,1:T(8,128)}, u32[]{:S(2)}) copy-start(f32[64,8]{0,1:T(8,128)} %param.25) | copy-start | bytes 6148
  391.7 110.3 %all-to-all-start.1 = ((bf16[48,1,8,4096]{3,2,1,0:T(8,128)(2,1)}), bf16[48,1,8,4096]{3,2,1,0:T(8,128)(2,1)}, u32[]{:S(2)}, u32[]{:S(2)}) async-start(bf16[48,1,8,4096]{3,2,1,0:T(8,128)(2,1)} %fusion), calls=%async_computation.1 | async-start | bytes 6291456 | tf_op jit(solution)/shard_map/all_to_all | solution.py:117
  400.1 230.3 %all-reduce.6.cloned.1.call-start = ((), (), s32[]{:S(2)}) async-start(), calls=%async_computation.4 | async-start | bytes 2097152
Sparse Core Ops, SparseCore 0:
  10.9 117.2 all-gather.1
  135.4 124.9 all-reduce.3
  506.7 123.6 all-reduce.5
where the time goes:
time: 639 us
  waiting for transfers between devices  464 us (73%)
  blocking collectives  119 us (19%)
  matrix products  14.9 us (2%)
  between operations  14 us (2%)
  other arithmetic  10.9 us (2%)
  starting transfers between devices  8.53 us (1%)
  local copies, waits for them, and re-layouts  7 us (1%)
    psum x1, waiting for transfers between devices, body(): summed = lax.psum(partial_value, 'exp')  125 us
    unnamed x4, waiting for transfers between devices  122 us
    all_to_all x1, blocking collectives, body(): lax.all_to_all(outgoing, 'ctx', split_axis=0, concat_axis=0, tiled=True)  119 us
    all_gather x1, waiting for transfers between devices, body(): piece = lax.all_gather(paired, 'ctx', axis=1, tiled=True)  116 us
    all_to_all x1, waiting for transfers between devices, body(): lax.all_to_all(pieces, 'ctx', split_axis=0, concat_axis=0, tiled=True)  102 us
  transfers between devices with their start and end apart: 4, of which 4 were waited for; matrix products, arithmetic and copies ran while one was open for 1% of the time, Pallas kernels for 0%

commit v1 on v0

v1 whole, which is shorter than its diff:
```python
import jax
import jax.numpy as jnp
import numpy as np
from jax import lax
from jax.sharding import Mesh
from jax.sharding import PartitionSpec as P

QUERY_HEADS = 64
KEY_VALUE_HEADS = 4
EXPERTS = 128
SLICES = 6
CAP = 8
THETA = 1000000.0
CTX = ("z", "x")
EXP = ("y", "core")


def apply_norm(value_rows, gain):
    mean_square = jnp.mean(value_rows * value_rows, axis=-1, keepdims=True)
    return value_rows * lax.rsqrt(mean_square + 1e-06) * gain


def apply_rotation(value_rows, token_positions):
    half = value_rows.shape[-1] // 2
    inverse = THETA ** (-(jnp.arange(half, dtype=jnp.float32) * 2.0 / value_rows.shape[-1]))
    angle = token_positions.astype(jnp.float32)[:, None] * inverse[None, :]
    cosine = jnp.cos(angle)[:, None, :]
    sine = jnp.sin(angle)[:, None, :]
    first = value_rows[..., :half]
    second = value_rows[..., half:]
    return jnp.concatenate(
        [first * cosine - second * sine, second * cosine + first * sine], axis=-1
    )


def sum_over_exp(partial, n_exp):
    terms = partial.astype(jnp.bfloat16).reshape(n_exp, partial.shape[0] // n_exp, -1)
    terms = lax.all_to_all(terms, EXP, split_axis=0, concat_axis=0, tiled=True)
    return jnp.sum(terms.astype(jnp.float32), axis=0)


def body(
    residual_in,
    queries,
    projected_key_value,
    query_gain,
    key_norm_gain,
    output_weight,
    norm_gain,
    gate_weight,
    up_weight,
    down_weight,
    expert_index,
    expert_slot,
    route_weight,
):
    rows = queries.shape[0]
    head_dim = query_gain.shape[0]
    local_heads = queries.shape[1] // head_dim
    n_x = lax.axis_size("x")
    n_z = lax.axis_size("z")
    n_ctx = n_x * n_z
    n_exp = lax.axis_size("y") * lax.axis_size("core")
    core = lax.axis_index("core")
    ctx_index = lax.axis_index("z") * n_x + lax.axis_index("x")
    exp_index = lax.axis_index("y") * 2 + core

    pair = [(c, c ^ 1) for c in range(n_ctx)]
    gate_other = lax.ppermute(gate_weight, CTX, pair)
    up_other = lax.ppermute(up_weight, CTX, pair)
    down_other = lax.ppermute(down_weight, CTX, pair)

    token_positions = ctx_index * rows + jnp.arange(rows, dtype=jnp.int32)
    key_value_head = exp_index * local_heads // (QUERY_HEADS // KEY_VALUE_HEADS)
    kv_block = lax.dynamic_slice_in_dim(projected_key_value, key_value_head * head_dim, head_dim, 2)
    rotated_keys = apply_rotation(
        apply_norm(kv_block[0].astype(jnp.float32)[:, None, :], key_norm_gain), token_positions
    )[:, 0, :].astype(jnp.bfloat16)
    mine = jnp.where(core == 0, rotated_keys, kv_block[1])
    mine = lax.all_gather(mine[None], "z", axis=0, tiled=True)
    mine = lax.all_gather(mine[None], "x", axis=0, tiled=True)
    mine = mine.reshape(n_ctx * rows, head_dim)
    other = lax.ppermute(mine, "core", [(0, 1), (1, 0)])
    keys = jnp.where(core == 0, mine, other)
    values = jnp.where(core == 0, other, mine)
    key_pos = (
        jnp.arange(n_z, dtype=jnp.int32)[None, :, None] * (n_x * rows)
        + jnp.arange(n_x, dtype=jnp.int32)[:, None, None] * rows
        + jnp.arange(rows, dtype=jnp.int32)[None, None, :]
    ).reshape(n_ctx * rows)

    query_rot = apply_rotation(
        apply_norm(queries.reshape(rows, local_heads, head_dim).astype(jnp.float32), query_gain),
        token_positions,
    ).astype(jnp.bfloat16)
    scale = 1.0 / head_dim**0.5
    scores = jnp.einsum("qhd,kd->hqk", query_rot, keys, preferred_element_type=jnp.float32) * scale
    visible = (key_pos[None, :] <= token_positions[:, None])[None, :, :]
    peak = jnp.max(jnp.where(visible, scores, -1e30), axis=-1)
    weights = jnp.where(visible, jnp.exp(scores - peak[..., None]), 0.0)
    total = jnp.sum(weights, axis=-1)
    accum = jnp.einsum(
        "hqk,kd->hqd", weights.astype(jnp.bfloat16), values, preferred_element_type=jnp.float32
    )
    attended = (
        jnp.transpose(accum / total[..., None], (1, 0, 2))
        .astype(jnp.bfloat16)
        .reshape(rows, local_heads * head_dim)
    )
    partial_value = jnp.dot(attended, output_weight, preferred_element_type=jnp.float32)
    share = rows // n_exp
    own_residual = lax.dynamic_slice_in_dim(residual_in, exp_index * share, share, 0)
    own_stream = own_residual.astype(jnp.float32) + sum_over_exp(partial_value, n_exp)
    own_normed = apply_norm(own_stream, norm_gain).astype(jnp.bfloat16)
    normed = lax.all_gather(own_normed, EXP, axis=0, tiled=True)

    local = EXPERTS // n_exp
    lanes = local * CAP
    local_expert = expert_index - exp_index * local
    owned = (local_expert >= 0) & (local_expert < local)
    target = jnp.where(owned, local_expert * CAP + expert_slot, -1)
    match = target[:, :, None] == jnp.arange(lanes, dtype=jnp.int32)[None, None, :]
    select = jnp.any(match, axis=1).astype(jnp.bfloat16)
    packed = lax.dot_general(
        select, normed, (((0,), (0,)), ((), ())), preferred_element_type=jnp.float32
    ).astype(jnp.bfloat16)
    combine_weights = jnp.sum(jnp.where(match, route_weight[:, :, None], 0.0), axis=1)

    pairs, half = SLICES // 2, CAP // 2
    width = packed.shape[-1]
    outgoing = jnp.broadcast_to(
        packed.reshape(local, 1, 2, half, width), (local, pairs, 2, half, width)
    ).reshape(n_ctx, half, width)
    arrived = lax.all_to_all(outgoing, CTX, split_axis=0, concat_axis=0, tiled=True)
    arrived = arrived.reshape(n_ctx * half, width)

    def hidden(gate_part, up_part):
        gate = jnp.dot(arrived, gate_part, preferred_element_type=jnp.float32)
        upper = jnp.dot(arrived, up_part, preferred_element_type=jnp.float32)
        return (jax.nn.silu(gate) * upper).astype(jnp.bfloat16)

    pieces = jnp.dot(
        hidden(gate_weight[0], up_weight[0]), down_weight[0], preferred_element_type=jnp.float32
    ) + jnp.dot(
        hidden(gate_other[0], up_other[0]), down_other[0], preferred_element_type=jnp.float32
    )
    pieces = pieces.astype(jnp.bfloat16).reshape(n_ctx, half, width)
    returned = lax.all_to_all(pieces, CTX, split_axis=0, concat_axis=0, tiled=True)
    expert_out = jnp.sum(
        returned.reshape(local, pairs, 2, half, width).astype(jnp.float32), axis=1
    ).reshape(lanes, width)
    mixture = jnp.dot(
        combine_weights,
        expert_out,
        precision=lax.Precision.HIGHEST,
        preferred_element_type=jnp.float32,
    )
    return (own_stream + sum_over_exp(mixture, n_exp)).astype(jnp.bfloat16)


def solution(mesh):
    shape = (12, 4, 8, 2)
    fine = Mesh(np.asarray(mesh.devices).reshape(shape), CTX + EXP)
    in_specs = (
        P(CTX, None),
        P(CTX, EXP),
        P(None, CTX, None),
        P(),
        P(),
        P(EXP, None),
        P(),
        P(EXP + CTX, None, None),
        P(EXP + CTX, None, None),
        P(EXP + CTX, None, None),
        P(CTX, None),
        P(CTX, None),
        P(CTX, None),
    )
    out_specs = P(CTX + EXP, None)
    return jax.shard_map(body, mesh=fine, in_specs=in_specs, out_specs=out_specs, check_vma=False)
```

time: 639 us -> 301 us (0.47)
  waiting for transfers between devices: 464 us -> 143 us
  blocking collectives: 119 us -> 81.5 us
  starting transfers between devices: 8.53 us -> 44.1 us
  between operations: 14 us -> 0.37 us
    psum x1 -> x0, waiting for transfers between devices: 125 us -> none  [body(): summed = lax.psum(partial_value, 'exp')]
    unnamed x4 -> x0, waiting for transfers between devices: 122 us -> none
    all_gather x1 -> x0, waiting for transfers between devices: 116 us -> none  [body(): piece = lax.all_gather(paired, 'ctx', axis=1, tiled=True)]
    all_to_all x1, blocking collectives: 119 us -> 25.9 us  [sum_over_exp(): terms = lax.all_to_all(terms, EXP, split_axis=0, concat_axis=0, tiled=True)]
    all_gather x0 -> x3, blocking collectives: none -> 55.6 us  [the longest x1 28.6 us: body(): mine = lax.all_gather(mine[None], 'z', axis=0, tiled=True)]
    ppermute x0 -> x4, waiting for transfers between devices: none -> 22.2 us  [the longest x1 21.4 us: body(): down_other = lax.ppermute(down_weight, CTX, pair)]
    ppermute x0 -> x4, starting transfers between devices: none -> 19 us  [the longest x1 10.7 us: body(): other = lax.ppermute(mine, 'core', [(0, 1), (1, 0)])]
    all_to_all x1 -> x3, waiting for transfers between devices: 102 us -> 120 us  [the longest x1 55 us: body(): lax.all_to_all(pieces, CTX, split_axis=0, concat_axis=0, tiled=True)]
  transfers between devices with their start and end apart: 4 -> 7, of which waited for: 4 -> 5; matrix products, arithmetic and copies ran while one was open for 1% -> 3% of each run, Pallas kernels for 0% -> 0%
where the time goes in v1:
time: 301 us; the launch traced here: 300 us
  waiting for transfers between devices  143 us (48%)
  blocking collectives  81.5 us (27%)
  starting transfers between devices  44.1 us (15%)
  matrix products  14.9 us (5%)
  other arithmetic  9.88 us (3%)
  local copies, waits for them, and re-layouts  7.03 us (2%)
    all_to_all x1, waiting for transfers between devices, body(): lax.all_to_all(pieces, CTX, split_axis=0, concat_axis=0, tiled=True)  55 us
    all_to_all x1, waiting for transfers between devices, body(): lax.all_to_all(outgoing, CTX, split_axis=0, concat_axis=0, tiled=True)  48.4 us
    all_gather x1, blocking collectives, body(): mine = lax.all_gather(mine[None], 'z', axis=0, tiled=True)  28.6 us
    all_to_all x1, blocking collectives, sum_over_exp(): terms = lax.all_to_all(terms, EXP, split_axis=0, concat_axis=0, tiled=True)  25.9 us
    ppermute x1, waiting for transfers between devices, body(): down_other = lax.ppermute(down_weight, CTX, pair)  21.4 us
    all_to_all x1, waiting for transfers between devices, sum_over_exp(): terms = lax.all_to_all(terms, EXP, split_axis=0, concat_axis=0, tiled=True)  17 us
    all_gather x1, blocking collectives, body(): normed = lax.all_gather(own_normed, EXP, axis=0, tiled=True)  15.9 us
    all_to_all x1, starting transfers between devices, body(): lax.all_to_all(pieces, CTX, split_axis=0, concat_axis=0, tiled=True)  12.3 us
  transfers between devices with their start and end apart: 7, of which 5 were waited for; matrix products, arithmetic and copies ran while one was open for 3% of the time, Pallas kernels for 0%

profile of v1, /device:TPU:1, one launch (start us, length us, event | category | flops | bytes accessed | tf_op | source)
XLA Modules:
  0.0 300.3 jit_solution(5219610509517331876)
XLA Ops:
  2.7 28.6 %all_gather.9 = bf16[12,64,128]{2,1,0:T(8,128)(2,1)S(1)} all-gather(bf16[1,64,128]{2,1,0:T(8,128)(2,1)S(1)} %dynamic-slice_select_fusion), channel_id=1, replica_groups=mesh['z'=12,'x'=4,'y'=8,'core'=2] {'z'}, dimensions={0}, use_global_device_ids=true | all-gather | bytes 212992 | tf_op jit(solution)/shard_map/all_gather | solution.py:80
  31.4 11.1 %all-gather = bf16[48,64,128]{2,1,0:T(8,128)(2,1)S(1)} all-gather(bf16[12,64,128]{2,1,0:T(8,128)(2,1)S(1)} %all_gather.9), channel_id=2, replica_groups=mesh['z'=12,'x'=4,'y'=8,'core'=2] {'x'}, dimensions={0}, use_global_device_ids=true | all-gather | bytes 983040 | tf_op jit(solution)/shard_map/all_gather | solution.py:81
  42.4 10.7 %collective-permute-start = (bf16[3072,128]{1,0:T(8,128)(2,1)S(1)}, bf16[3072,128]{1,0:T(8,128)(2,1)S(1)}, u32[]{:S(2)}, u32[]{:S(2)}) collective-permute-start(bf16[3072,128]{1,0:T(8,128)(2,1)S(1)} %bitcast.80), channel_id=1, source_target_pairs={{0,1},{1,0},{2,3},{3,2},{4,5},{5,4},{6,7},{7,6},{8,9},{9,8},{10,11... | collective-permute-start | bytes 2359304 | tf_op jit(solution)/shard_map/ppermute | solution.py:83
  55.6 1.1 fusion.79
  59.7 7.5 %all-to-all-start = ((bf16[16,4,4096]{2,1,0:T(4,128)(2,1)}), bf16[16,4,4096]{2,1,0:T(4,128)(2,1)S(1)}, u32[]{:S(2)}, u32[]{:S(2)}) async-start(bf16[16,4,4096]{2,1,0:T(4,128)(2,1)} %reshape.336), calls=%async_computation | async-start | bytes 1048576 | tf_op jit(solution)/shard_map/all_to_all | solution.py:38
  67.5 17.0 %all-to-all-done = bf16[16,4,4096]{2,1,0:T(4,128)(2,1)S(1)} async-done(((bf16[16,4,4096]{2,1,0:T(4,128)(2,1)}), bf16[16,4,4096]{2,1,0:T(4,128)(2,1)S(1)}, u32[]{:S(2)}, u32[]{:S(2)}) %all-to-all-start) | async-done | bytes 524320 | tf_op jit(solution)/shard_map/all_to_all | solution.py:38
  86.6 15.9 %all-gather.1 = bf16[16,4,4096]{2,1,0:T(4,128)(2,1)S(1)} all-gather(bf16[1,4,4096]{2,1,0:T(4,128)(2,1)S(1)} %fusion.73), channel_id=1, replica_groups=mesh['z'=12,'x'=4,'y'=8,'core'=2] {'y','core'}, dimensions={0}, use_global_device_ids=true | all-gather | bytes 557056 | tf_op jit(solution)/shard_map/all_gather | solution.py:115
  103.2 1.9 broadcast_in_dim.78
  105.1 5.3 %all-to-all-start.1 = ((bf16[48,4,4096]{2,1,0:T(4,128)(2,1)}), bf16[48,4,4096]{2,1,0:T(4,128)(2,1)S(1)}, u32[]{:S(2)}, u32[]{:S(2)}) async-start(bf16[48,4,4096]{2,1,0:T(4,128)(2,1)} %bitcast.10), calls=%async_computation.1 | async-start | bytes 3145728 | tf_op jit(solution)/shard_map/all_to_all | solution.py:134
  110.4 3.0 %collective-permute-start.2 = (bf16[1,4096,128]{2,1,0:T(8,128)(2,1)}, bf16[1,4096,128]{2,1,0:T(8,128)(2,1)}, u32[]{:S(2)}, u32[]{:S(2)}) collective-permute-start(bf16[1,4096,128]{2,1,0:T(8,128)(2,1)} %param.21), channel_id=1, source_target_pairs={{0,16},{16,0},{32,48},{48,32},{64,80},{80,64},{96,112},{112,96},{1... | collective-permute-start | bytes 3145736 | tf_op jit(solution)/shard_map/ppermute | solution.py:70
  113.5 2.3 collective-permute-start.1
  115.7 3.0 %collective-permute-start.3 = (bf16[1,128,4096]{2,1,0:T(8,128)(2,1)}, bf16[1,128,4096]{2,1,0:T(8,128)(2,1)}, u32[]{:S(2)}, u32[]{:S(2)}) collective-permute-start(bf16[1,128,4096]{2,1,0:T(8,128)(2,1)} %param.22), channel_id=1, source_target_pairs={{0,16},{16,0},{32,48},{48,32},{64,80},{80,64},{96,112},{112,96},{1... | collective-permute-start | bytes 3145736 | tf_op jit(solution)/shard_map/ppermute | solution.py:71
  118.8 48.4 %all-to-all-done.1 = bf16[48,4,4096]{2,1,0:T(4,128)(2,1)S(1)} async-done(((bf16[48,4,4096]{2,1,0:T(4,128)(2,1)}), bf16[48,4,4096]{2,1,0:T(4,128)(2,1)S(1)}, u32[]{:S(2)}, u32[]{:S(2)}) %all-to-all-start.1) | async-done | bytes 1572896 | tf_op jit(solution)/shard_map/all_to_all | solution.py:134
  167.5 1.8 fusion.37
  169.3 1.8 fusion.30
  171.1 4.3 %fusion.28 = f32[192,4096]{1,0:T(8,128)} fusion(bf16[192,4096]{1,0:T(8,128)(2,1)S(1)} %reshape.338, bf16[1,128,4096]{2,1,0:T(8,128)(2,1)} %param.22, bf16[1,4096,128]{2,1,0:T(8,128)(2,1)} %param.21, f32[192,128]{1,0:T(8,128)S(1)} %fusion.37), kind=kOutput, calls=%fused_computation.24 | convolution fusion | flops 402800640 | bytes 6914048 | tf_op jit(solution)/shard_map/dot_general | solution.py:142
  175.4 21.4 %collective-permute-done.3 = bf16[1,128,4096]{2,1,0:T(8,128)(2,1)} collective-permute-done((bf16[1,128,4096]{2,1,0:T(8,128)(2,1)}, bf16[1,128,4096]{2,1,0:T(8,128)(2,1)}, u32[]{:S(2)}, u32[]{:S(2)}) %collective-permute-start.3) | collective-permute-done | bytes 1048608 | tf_op jit(solution)/shard_map/ppermute | solution.py:71
  196.8 3.6 %fusion.1 = bf16[192,4096]{1,0:T(8,128)(2,1)S(1)} fusion(f32[192,4096]{1,0:T(8,128)} %fusion.28, bf16[1,128,4096]{2,1,0:T(8,128)(2,1)} %collective-permute-done.3, f32[192,128]{1,0:T(8,128)S(1)} %fusion.30, bf16[192,4096]{1,0:T(8,128)(2,1)S(1)} %reshape.338, bf16[1,4096,128]{2,1,0:T(8,128)(2,1)} %collective-permute-done.1), kind=kOutput, calls=%fused_computation.2 | convolution fusion | flops 404373504 | bytes 8486912 | tf_op jit(solution)/shard_map/dot_general | solution.py:144
  200.5 2.0 reshape.339
  202.5 12.3 %all-to-all-start.2 = ((bf16[48,4,4096]{2,1,0:T(4,128)(2,1)}), bf16[48,4,4096]{2,1,0:T(4,128)(2,1)S(1)}, u32[]{:S(2)}, u32[]{:S(2)}) async-start(bf16[48,4,4096]{2,1,0:T(4,128)(2,1)} %reshape.339), calls=%async_computation.2 | async-start | bytes 3145728 | tf_op jit(solution)/shard_map/all_to_all | solution.py:148
  215.1 55.0 %all-to-all-done.2 = bf16[48,4,4096]{2,1,0:T(4,128)(2,1)S(1)} async-done(((bf16[48,4,4096]{2,1,0:T(4,128)(2,1)}), bf16[48,4,4096]{2,1,0:T(4,128)(2,1)S(1)}, u32[]{:S(2)}, u32[]{:S(2)}) %all-to-all-start.2) | async-done | bytes 1572896 | tf_op jit(solution)/shard_map/all_to_all | solution.py:148
  271.5 1.0 convolution_convert_fusion.1
  272.7 25.9 %all_to_all.20 = bf16[16,4,4096]{2,1,0:T(4,128)(2,1)S(1)} all-to-all(bf16[16,4,4096]{2,1,0:T(4,128)(2,1)S(1)} %reshape.341), channel_id=1, replica_groups=mesh['z'=12,'x'=4,'y'=8,'core'=2] {'y','core'}, dimensions={0} | all-to-all | bytes 1048576 | tf_op jit(solution)/shard_map/all_to_all | solution.py:38
  298.8 1.5 add_convert_fusion.1
  (59 shorter events, 13.6 us)
Async XLA Ops:
  0.0 53.3 %copy-start.1 = (bf16[64,512]{1,0:T(8,128)(2,1)S(1)}, bf16[64,512]{1,0:T(8,128)(2,1)}, u32[]{:S(2)}) copy-start(bf16[64,512]{1,0:T(8,128)(2,1)} %param.14) | copy-start | bytes 196612
  0.0 53.8 %copy-start.6 = (f32[128]{0:T(128)S(1)}, f32[128]{0:T(128)}, u32[]{:S(2)}) copy-start(f32[128]{0:T(128)} %param.16) | copy-start | bytes 1540
  42.4 12.6 %collective-permute-start = (bf16[3072,128]{1,0:T(8,128)(2,1)S(1)}, bf16[3072,128]{1,0:T(8,128)(2,1)S(1)}, u32[]{:S(2)}, u32[]{:S(2)}) collective-permute-start(bf16[3072,128]{1,0:T(8,128)(2,1)S(1)} %bitcast.80), channel_id=1, source_target_pairs={{0,1},{1,0},{2,3},{3,2},{4,5},{5,4},{6,7},{7,6},{8,9},{9,8},{10,11... | collective-permute-start | bytes 2359304 | tf_op jit(solution)/shard_map/ppermute | solution.py:83
  55.6 2.2 copy-start
  58.7 8.5 %copy-start.3 = (s32[64,8]{0,1:T(8,128)S(1)}, s32[64,8]{0,1:T(8,128)}, u32[]{:S(2)}) copy-start(s32[64,8]{0,1:T(8,128)} %param.24) | copy-start | bytes 6148
  58.7 8.5 %copy-start.4 = (s32[64,8]{0,1:T(8,128)S(1)}, s32[64,8]{0,1:T(8,128)}, u32[]{:S(2)}) copy-start(s32[64,8]{0,1:T(8,128)} %param.23) | copy-start | bytes 6148
  58.7 27.0 %copy-start.2 = (f32[4096]{0:T(1024)S(1)}, f32[4096]{0:T(1024)}, u32[]{:S(2)}) copy-start(f32[4096]{0:T(1024)} %param.19) | copy-start | bytes 49156
  59.7 24.8 %all-to-all-start = ((bf16[16,4,4096]{2,1,0:T(4,128)(2,1)}), bf16[16,4,4096]{2,1,0:T(4,128)(2,1)S(1)}, u32[]{:S(2)}, u32[]{:S(2)}) async-start(bf16[16,4,4096]{2,1,0:T(4,128)(2,1)} %reshape.336), calls=%async_computation | async-start | bytes 1048576 | tf_op jit(solution)/shard_map/all_to_all | solution.py:38
  105.1 62.0 %all-to-all-start.1 = ((bf16[48,4,4096]{2,1,0:T(4,128)(2,1)}), bf16[48,4,4096]{2,1,0:T(4,128)(2,1)S(1)}, u32[]{:S(2)}, u32[]{:S(2)}) async-start(bf16[48,4,4096]{2,1,0:T(4,128)(2,1)} %bitcast.10), calls=%async_computation.1 | async-start | bytes 3145728 | tf_op jit(solution)/shard_map/all_to_all | solution.py:134
  110.4 58.9 %collective-permute-start.2 = (bf16[1,4096,128]{2,1,0:T(8,128)(2,1)}, bf16[1,4096,128]{2,1,0:T(8,128)(2,1)}, u32[]{:S(2)}, u32[]{:S(2)}) collective-permute-start(bf16[1,4096,128]{2,1,0:T(8,128)(2,1)} %param.21), channel_id=1, source_target_pairs={{0,16},{16,0},{32,48},{48,32},{64,80},{80,64},{96,112},{112,96},{1... | collective-permute-start | bytes 3145736 | tf_op jit(solution)/shard_map/ppermute | solution.py:70
  113.5 61.9 %collective-permute-start.1 = (bf16[1,4096,128]{2,1,0:T(8,128)(2,1)}, bf16[1,4096,128]{2,1,0:T(8,128)(2,1)}, u32[]{:S(2)}, u32[]{:S(2)}) collective-permute-start(bf16[1,4096,128]{2,1,0:T(8,128)(2,1)} %param.20), channel_id=1, source_target_pairs={{0,16},{16,0},{32,48},{48,32},{64,80},{80,64},{96,112},{112,96},{1... | collective-permute-start | bytes 3145736 | tf_op jit(solution)/shard_map/ppermute | solution.py:69
  115.7 81.1 %collective-permute-start.3 = (bf16[1,128,4096]{2,1,0:T(8,128)(2,1)}, bf16[1,128,4096]{2,1,0:T(8,128)(2,1)}, u32[]{:S(2)}, u32[]{:S(2)}) collective-permute-start(bf16[1,128,4096]{2,1,0:T(8,128)(2,1)} %param.22), channel_id=1, source_target_pairs={{0,16},{16,0},{32,48},{48,32},{64,80},{80,64},{96,112},{112,96},{1... | collective-permute-start | bytes 3145736 | tf_op jit(solution)/shard_map/ppermute | solution.py:71
  202.5 12.3 %copy-start.5 = (f32[64,8]{0,1:T(8,128)S(1)}, f32[64,8]{0,1:T(8,128)}, u32[]{:S(2)}) copy-start(f32[64,8]{0,1:T(8,128)} %param.25) | copy-start | bytes 6148
  202.5 67.7 %all-to-all-start.2 = ((bf16[48,4,4096]{2,1,0:T(4,128)(2,1)}), bf16[48,4,4096]{2,1,0:T(4,128)(2,1)S(1)}, u32[]{:S(2)}, u32[]{:S(2)}) async-start(bf16[48,4,4096]{2,1,0:T(4,128)(2,1)} %reshape.339), calls=%async_computation.2 | async-start | bytes 3145728 | tf_op jit(solution)/shard_map/all_to_all | solution.py:148

commit v2 on v1

--- a/solution.py
+++ b/solution.py
@@ -2,6 +2,8 @@
 import jax.numpy as jnp
 import numpy as np
 from jax import lax
+from jax.experimental import pallas as pl
+from jax.experimental.pallas import tpu as pltpu
 from jax.sharding import Mesh
 from jax.sharding import PartitionSpec as P
 
@@ -33,10 +35,64 @@
     )
 
 
-def sum_over_exp(partial, n_exp):
-    terms = partial.astype(jnp.bfloat16).reshape(n_exp, partial.shape[0] // n_exp, -1)
-    terms = lax.all_to_all(terms, EXP, split_axis=0, concat_axis=0, tiled=True)
-    return jnp.sum(terms.astype(jnp.float32), axis=0)
+def sum_over_exp(partial, core):
+    n_y = lax.axis_size("y")
+    terms = partial.reshape(n_y, 2, partial.shape[0] // (2 * n_y), -1)
+    keep = lax.dynamic_index_in_dim(terms, core, 1, keepdims=False)
+    give = lax.dynamic_index_in_dim(terms, 1 - core, 1, keepdims=False).astype(jnp.bfloat16)
+    got = lax.ppermute(give, "core", [(0, 1), (1, 0)])
+    both = (keep + got.astype(jnp.float32)).astype(jnp.bfloat16)
+    both = lax.all_to_all(both, "y", split_axis=0, concat_axis=0, tiled=True)
+    return jnp.sum(both.astype(jnp.float32), axis=0)
+
+
+def expert_kernel(steps, x_ref, ga_ref, ua_ref, gb_ref, ub_ref, da_ref, db_ref, out_ref, sums):
+    step = pl.program_id(0)
+
+    @pl.when(step == 0)
+    def _():
+        sums[...] = jnp.zeros_like(sums)
+
+    x = x_ref[...]
+    for i, ref in enumerate((ga_ref, ua_ref, gb_ref, ub_ref)):
+        sums[i] += jnp.dot(x, ref[0], preferred_element_type=jnp.float32)
+
+    @pl.when(step == steps - 1)
+    def _():
+        acts = []
+        for i in (0, 2):
+            gate = sums[i]
+            acts.append((gate / (1.0 + jnp.exp(-gate)) * sums[i + 1]).astype(jnp.bfloat16))
+        columns = 1024
+        for j in range(out_ref.shape[1] // columns):
+            part = pl.ds(j * columns, columns)
+            out_ref[:, part] = (
+                jnp.dot(acts[0], da_ref[0, :, part], preferred_element_type=jnp.float32)
+                + jnp.dot(acts[1], db_ref[0, :, part], preferred_element_type=jnp.float32)
+            ).astype(jnp.bfloat16)
+
+
+def expert_pair(rows, gate_a, up_a, gate_b, up_b, down_a, down_b):
+    count, width = rows.shape
+    hidden = gate_a.shape[-1]
+    steps = 8
+    depth = width // steps
+    into = pl.BlockSpec((1, depth, hidden), lambda k: (0, k, 0))
+    back = pl.BlockSpec((1, hidden, width), lambda k: (0, 0, 0))
+    return pl.pallas_call(
+        lambda *refs: expert_kernel(steps, *refs),
+        grid=(steps,),
+        in_specs=[pl.BlockSpec((count, depth), lambda k: (0, k)), into, into, into, into, back, back],
+        out_specs=pl.BlockSpec((count, width), lambda k: (0, 0)),
+        out_shape=jax.ShapeDtypeStruct((count, width), jnp.bfloat16),
+        scratch_shapes=[pltpu.VMEM((4, count, hidden), jnp.float32)],
+        compiler_params=pltpu.CompilerParams(vmem_limit_bytes=32 * 1024 * 1024),
+        cost_estimate=pl.CostEstimate(
+            flops=12 * count * width * hidden,
+            bytes_accessed=4 * count * width + 12 * width * hidden,
+            transcendentals=2 * count * hidden,
+        ),
+    )(rows, gate_a, up_a, gate_b, up_b, down_a, down_b)
 
 
 def body(
@@ -78,6 +134,7 @@
     )[:, 0, :].astype(jnp.bfloat16)
     mine = jnp.where(core == 0, rotated_keys, kv_block[1])
     mine = lax.all_gather(mine[None], "z", axis=0, tiled=True)
+    mine, gate_other = lax.optimization_barrier((mine, gate_other))
     mine = lax.all_gather(mine[None], "x", axis=0, tiled=True)
     mine = mine.reshape(n_ctx * rows, head_dim)
     other = lax.ppermute(mine, "core", [(0, 1), (1, 0)])
@@ -110,52 +167,44 @@
     partial_value = jnp.dot(attended, output_weight, preferred_element_type=jnp.float32)
     share = rows // n_exp
     own_residual = lax.dynamic_slice_in_dim(residual_in, exp_index * share, share, 0)
-    own_stream = own_residual.astype(jnp.float32) + sum_over_exp(partial_value, n_exp)
+    own_stream = own_residual.astype(jnp.float32) + sum_over_exp(partial_value, core)
+    own_stream, up_other = lax.optimization_barrier((own_stream, up_other))
     own_normed = apply_norm(own_stream, norm_gain).astype(jnp.bfloat16)
     normed = lax.all_gather(own_normed, EXP, axis=0, tiled=True)
 
     local = EXPERTS // n_exp
-    lanes = local * CAP
-    local_expert = expert_index - exp_index * local
-    owned = (local_expert >= 0) & (local_expert < local)
-    target = jnp.where(owned, local_expert * CAP + expert_slot, -1)
-    match = target[:, :, None] == jnp.arange(lanes, dtype=jnp.int32)[None, None, :]
+    pairs, half = SLICES // 2, CAP // 2
+    lanes = n_ctx * half
+    lane = jnp.arange(lanes, dtype=jnp.int32)
+    lane_expert = lane // (pairs * CAP) + exp_index * local
+    lane_slot = lane // half % 2 * half + lane % half
+    match = (expert_index[:, :, None] == lane_expert) & (expert_slot[:, :, None] == lane_slot)
     select = jnp.any(match, axis=1).astype(jnp.bfloat16)
-    packed = lax.dot_general(
+    combine = jnp.sum(jnp.where(match, route_weight[:, :, None], 0.0), axis=1)
+    combine_high = combine.astype(jnp.bfloat16)
+    combine_low = (combine - combine_high.astype(jnp.float32)).astype(jnp.bfloat16)
+
+    outgoing = lax.dot_general(
         select, normed, (((0,), (0,)), ((), ())), preferred_element_type=jnp.float32
     ).astype(jnp.bfloat16)
-    combine_weights = jnp.sum(jnp.where(match, route_weight[:, :, None], 0.0), axis=1)
-
-    pairs, half = SLICES // 2, CAP // 2
-    width = packed.shape[-1]
-    outgoing = jnp.broadcast_to(
-        packed.reshape(local, 1, 2, half, width), (local, pairs, 2, half, width)
+    width = normed.shape[-1]
+    outgoing = outgoing.reshape(n_ctx, half, width)
+    arrived = lax.all_to_all(outgoing, CTX, split_axis=0, concat_axis=0, tiled=True)
+    pieces = expert_pair(
+        arrived.reshape(lanes, width),
+        gate_weight,
+        up_weight,
+        gate_other,
+        up_other,
+        down_weight,
+        down_other,
     ).reshape(n_ctx, half, width)
-    arrived = lax.all_to_all(outgoing, CTX, split_axis=0, concat_axis=0, tiled=True)
-    arrived = arrived.reshape(n_ctx * half, width)
-
-    def hidden(gate_part, up_part):
-        gate = jnp.dot(arrived, gate_part, preferred_element_type=jnp.float32)
-        upper = jnp.dot(arrived, up_part, preferred_element_type=jnp.float32)
-        return (jax.nn.silu(gate) * upper).astype(jnp.bfloat16)
-
-    pieces = jnp.dot(
-        hidden(gate_weight[0], up_weight[0]), down_weight[0], preferred_element_type=jnp.float32
-    ) + jnp.dot(
-        hidden(gate_other[0], up_other[0]), down_other[0], preferred_element_type=jnp.float32
-    )
-    pieces = pieces.astype(jnp.bfloat16).reshape(n_ctx, half, width)
     returned = lax.all_to_all(pieces, CTX, split_axis=0, concat_axis=0, tiled=True)
-    expert_out = jnp.sum(
-        returned.reshape(local, pairs, 2, half, width).astype(jnp.float32), axis=1
-    ).reshape(lanes, width)
-    mixture = jnp.dot(
-        combine_weights,
-        expert_out,
-        precision=lax.Precision.HIGHEST,
-        preferred_element_type=jnp.float32,
-    )
-    return (own_stream + sum_over_exp(mixture, n_exp)).astype(jnp.bfloat16)
+    returned = returned.reshape(lanes, width)
+    mixture = jnp.dot(combine_high, returned, preferred_element_type=jnp.float32) + jnp.dot(
+        combine_low, returned, preferred_element_type=jnp.float32
+    )
+    return (own_stream + sum_over_exp(mixture, core)).astype(jnp.bfloat16)
 
 
 def solution(mesh):

time: 301 us -> 300 us (level)
  local copies, waits for them, and re-layouts: 7.03 us -> 18.1 us
  waiting for transfers between devices: 143 us -> 134 us
  blocking collectives: 81.5 us -> 73.6 us
  Pallas kernels: 0 us -> 5.3 us
  starting transfers between devices: 44.1 us -> 49.2 us
  matrix products: 14.9 us -> 10.2 us
    ppermute x1, waiting for transfers between devices: 21.4 us -> 0.01 us  [body(): down_other = lax.ppermute(down_weight, CTX, pair)]
    ppermute x1, waiting for transfers between devices: 0.01 us -> 13.9 us  [body(): up_other = lax.ppermute(up_weight, CTX, pair)]
    dot_general x5 -> x2, matrix products: 12.5 us -> 0.81 us  [the longest x1 0.41 us: body(): jnp.dot(combine_low, returned, preferred_element_type=jnp.float32)]
    all_to_all x1, blocking collectives: 25.9 us -> 15.1 us  [sum_over_exp(): both = lax.all_to_all(both, 'y', split_axis=0, concat_axis=0, tiled=True)]
    ppermute x0 -> x2, starting transfers between devices: none -> 9.27 us  [sum_over_exp(): got = lax.ppermute(give, 'core', [(0, 1), (1, 0)])]
    all_to_all x1, waiting for transfers between devices: 17 us -> 8.14 us  [sum_over_exp(): both = lax.all_to_all(both, 'y', split_axis=0, concat_axis=0, tiled=True)]
    unnamed x16 -> x32, local copies, waits for them, and re-layouts: 0.71 us -> 7.12 us
    pallas_call x0 -> x1, Pallas kernels: none -> 5.3 us  [expert_pair(): pl.pallas_call(lambda *refs: expert_kernel(steps, *refs), grid=(steps,),...]
  transfers between devices with their start and end apart: 7 -> 9, of which waited for: 5 -> 7; matrix products, arithmetic and copies ran while one was open for 3% -> 3% of each run, Pallas kernels for 0% -> 0%
where the time goes in v2:
time: 300 us; the launch traced here: 299 us
  waiting for transfers between devices  134 us (45%)
  blocking collectives  73.6 us (25%)
  starting transfers between devices  49.2 us (16%)
  local copies, waits for them, and re-layouts  18.1 us (6%)
  matrix products  10.2 us (3%)
  other arithmetic  8.19 us (3%)
  Pallas kernels  5.3 us (2%)
    all_to_all x1, waiting for transfers between devices, body(): lax.all_to_all(pieces, CTX, split_axis=0, concat_axis=0, tiled=True)  53.9 us
    all_to_all x1, waiting for transfers between devices, body(): lax.all_to_all(outgoing, CTX, split_axis=0, concat_axis=0, tiled=True)  53.6 us
    all_gather x1, blocking collectives, body(): mine = lax.all_gather(mine[None], 'z', axis=0, tiled=True)  27.8 us
    all_gather x1, blocking collectives, body(): normed = lax.all_gather(own_normed, EXP, axis=0, tiled=True)  19.9 us
    all_to_all x1, blocking collectives, sum_over_exp(): both = lax.all_to_all(both, 'y', split_axis=0, concat_axis=0, tiled=True)  15.1 us
    ppermute x1, waiting for transfers between devices, body(): up_other = lax.ppermute(up_weight, CTX, pair)  13.9 us
    ppermute x1, starting transfers between devices, body(): other = lax.ppermute(mine, 'core', [(0, 1), (1, 0)])  11.1 us
    all_gather x1, blocking collectives, body(): mine = lax.all_gather(mine[None], 'x', axis=0, tiled=True)  10.8 us
  transfers between devices with their start and end apart: 9, of which 7 were waited for; matrix products, arithmetic and copies ran while one was open for 3% of the time, Pallas kernels for 0%

profile of v2, /device:TPU:1, one launch (start us, length us, event | category | flops | bytes accessed | tf_op | source)
XLA Modules:
  0.0 298.6 jit_solution(9467378403201746007)
XLA Ops:
  0.0 3.9 %collective-permute-start = (bf16[1,4096,128]{2,1,0:T(8,128)(2,1)}, bf16[1,4096,128]{2,1,0:T(8,128)(2,1)S(1)}, u32[]{:S(2)}, u32[]{:S(2)}) collective-permute-start(bf16[1,4096,128]{2,1,0:T(8,128)(2,1)} %refs_1_.1), channel_id=1, source_target_pairs={{0,16},{16,0},{32,48},{48,32},{64,80},{80,64},{96,112},{112,96},{1... | collective-permute-start | bytes 3145736 | tf_op jit(solution)/shard_map/ppermute | solution.py:125
  8.0 27.8 %all_gather.9 = bf16[12,64,128]{2,1,0:T(8,128)(2,1)S(1)} all-gather(bf16[1,64,128]{2,1,0:T(8,128)(2,1)S(1)} %dynamic-slice_select_fusion), channel_id=1, replica_groups=mesh['z'=12,'x'=4,'y'=8,'core'=2] {'z'}, dimensions={0}, use_global_device_ids=true | all-gather | bytes 212992 | tf_op jit(solution)/shard_map/all_gather | solution.py:136
  37.1 10.8 %all-gather = bf16[48,64,128]{2,1,0:T(8,128)(2,1)S(1)} all-gather(bf16[12,64,128]{2,1,0:T(8,128)(2,1)S(1)} %all_gather.9), channel_id=2, replica_groups=mesh['z'=12,'x'=4,'y'=8,'core'=2] {'x'}, dimensions={0}, use_global_device_ids=true | all-gather | bytes 983040 | tf_op jit(solution)/shard_map/all_gather | solution.py:138
  47.9 11.1 %collective-permute-start.1 = (bf16[3072,128]{1,0:T(8,128)(2,1)S(1)}, bf16[3072,128]{1,0:T(8,128)(2,1)S(1)}, u32[]{:S(2)}, u32[]{:S(2)}) collective-permute-start(bf16[3072,128]{1,0:T(8,128)(2,1)S(1)} %bitcast.57), channel_id=1, source_target_pairs={{0,1},{1,0},{2,3},{3,2},{4,5},{5,4},{6,7},{7,6},{8,9},{9,8},{10,11... | collective-permute-start | bytes 2359304 | tf_op jit(solution)/shard_map/ppermute | solution.py:140
  63.2 3.9 %fusion.22 = bf16[64,4,128]{2,0,1:T(8,128)(2,1)S(1)} fusion(bf16[3072,128]{1,0:T(8,128)(2,1)S(1)} %collective-permute-done.1, bf16[3072,128]{1,0:T(8,128)(2,1)S(1)} %bitcast.59, pred[]{:T(512)S(6)} %eq.17, f32[64,4]{0,1:T(4,128)S(1)} %bitcast.60, f32[4,64,3072]{2,1,0:T(8,128)} %copy-done.9, pred[64,3072]{1,0:T(8,128)(4,1)S(1)} %broadcast_compare_fusion), kind=kOutput, calls=%fused_computation.18 | convolution fusion | flops 204934400 | bytes 4981761 | tf_op jit(solution)/shard_map/hqk,kd->hqd/dot_general | solution.py:159
  67.3 3.1 %fusion.1 = f32[8,2,4,4096]{3,0,2,1:T(8,128)S(1)} fusion(bf16[512,4096]{1,0:T(8,128)(2,1)} %param.18, bf16[8,2,4,512]{3,2,1,0:T(4,128)(2,1)S(1)} %dot_general.25), kind=kOutput, calls=%fused_computation.3 | convolution fusion | flops 268435456 | bytes 5308416 | tf_op jit(solution)/shard_map/dot_general | solution.py:167
  70.5 2.3 collective-permute-start.2
  74.8 6.8 %all-to-all-start = ((bf16[8,4,4096]{2,1,0:T(4,128)(2,1)}), bf16[8,4,4096]{2,1,0:T(4,128)(2,1)S(1)}, u32[]{:S(2)}, u32[]{:S(2)}) async-start(bf16[8,4,4096]{2,1,0:T(4,128)(2,1)} %copy.43), calls=%async_computation | async-start | bytes 524288 | tf_op jit(solution)/shard_map/all_to_all | solution.py:45
  81.7 2.5 collective-permute-start.3
  84.6 8.1 %all-to-all-done = bf16[8,4,4096]{2,1,0:T(4,128)(2,1)S(1)} async-done(((bf16[8,4,4096]{2,1,0:T(4,128)(2,1)}), bf16[8,4,4096]{2,1,0:T(4,128)(2,1)S(1)}, u32[]{:S(2)}, u32[]{:S(2)}) %all-to-all-start) | async-done | bytes 262176 | tf_op jit(solution)/shard_map/all_to_all | solution.py:45
  93.7 13.9 %collective-permute-done.3.refs_4_ = bf16[1,4096,128]{2,1,0:T(8,128)(2,1)S(1)} collective-permute-done((bf16[1,4096,128]{2,1,0:T(8,128)(2,1)S(1)}, bf16[1,4096,128]{2,1,0:T(8,128)(2,1)S(1)}, u32[]{:S(2)}, u32[]{:S(2)}) %collective-permute-start.3) | collective-permute-done | bytes 1048608 | tf_op jit(solution)/shard_map/ppermute | solution.py:126
  107.9 19.9 %all-gather.1 = bf16[16,4,4096]{2,1,0:T(4,128)(2,1)S(1)} all-gather(bf16[1,4,4096]{2,1,0:T(4,128)(2,1)S(1)} %fusion.51), channel_id=1, replica_groups=mesh['z'=12,'x'=4,'y'=8,'core'=2] {'y','core'}, dimensions={0}, use_global_device_ids=true | all-gather | bytes 557056 | tf_op jit(solution)/shard_map/all_gather | solution.py:173
  127.9 1.8 convolution_convert_fusion
  129.6 3.7 %reshape.376 = bf16[48,4,4096]{2,1,0:T(4,128)(2,1)} reshape(bf16[192,4096]{1,0:T(8,128)(2,1)} %convolution_convert_fusion) | data formatting | bytes 3145728 | tf_op jit(solution)/shard_map/reshape | solution.py:191
  133.4 5.6 %all-to-all-start.1 = ((bf16[48,4,4096]{2,1,0:T(4,128)(2,1)}), bf16[48,4,4096]{2,1,0:T(4,128)(2,1)}, u32[]{:S(2)}, u32[]{:S(2)}) async-start(bf16[48,4,4096]{2,1,0:T(4,128)(2,1)} %reshape.376), calls=%async_computation.1 | async-start | bytes 3145728 | tf_op jit(solution)/shard_map/all_to_all | solution.py:192
  139.0 3.0 collective-permute-start.4
  141.9 53.6 %all-to-all-done.1 = bf16[48,4,4096]{2,1,0:T(4,128)(2,1)} async-done(((bf16[48,4,4096]{2,1,0:T(4,128)(2,1)}), bf16[48,4,4096]{2,1,0:T(4,128)(2,1)}, u32[]{:S(2)}, u32[]{:S(2)}) %all-to-all-start.1) | async-done | bytes 1572896 | tf_op jit(solution)/shard_map/all_to_all | solution.py:192
  195.6 2.4 reshape.377.refs_0_
  204.1 5.3 %shard_map.127 = bf16[192,4096]{1,0:T(8,128)(2,1)S(1)} custom-call(bf16[192,4096]{1,0:T(8,128)(2,1)S(1)} %reshape.377.refs_0_, bf16[1,4096,128]{2,1,0:T(8,128)(2,1)S(1)} %copy-done, bf16[1,4096,128]{2,1,0:T(8,128)(2,1)S(1)} %copy-done.2, bf16[1,4096,128]{2,1,0:T(8,128)(2,1)S(1)} %copy-done.6, bf16[1,4096,128]{2,1,0:T(8,128)(2,1)S(1)} %copy-done.8, ...), custom_call_target="tpu_custom_call" | custom-call | flops 1207959552 | bytes 9437184 | tf_op jit(solution)/shard_map/pallas_call | solution.py:82
  209.4 2.0 reshape.378
  211.4 7.1 %all-to-all-start.2 = ((bf16[48,4,4096]{2,1,0:T(4,128)(2,1)}), bf16[48,4,4096]{2,1,0:T(4,128)(2,1)S(1)}, u32[]{:S(2)}, u32[]{:S(2)}) async-start(bf16[48,4,4096]{2,1,0:T(4,128)(2,1)} %reshape.378), calls=%async_computation.2 | async-start | bytes 3145728 | tf_op jit(solution)/shard_map/all_to_all | solution.py:202
  218.9 53.9 %all-to-all-done.2 = bf16[48,4,4096]{2,1,0:T(4,128)(2,1)S(1)} async-done(((bf16[48,4,4096]{2,1,0:T(4,128)(2,1)}), bf16[48,4,4096]{2,1,0:T(4,128)(2,1)S(1)}, u32[]{:S(2)}, u32[]{:S(2)}) %all-to-all-start.2) | async-done | bytes 1572896 | tf_op jit(solution)/shard_map/all_to_all | solution.py:202
  274.4 7.0 %collective-permute-start.5 = (bf16[8,4,4096]{2,1,0:T(4,128)(2,1)S(1)}, bf16[8,4,4096]{2,1,0:T(4,128)(2,1)S(1)}, u32[]{:S(2)}, u32[]{:S(2)}) collective-permute-start(bf16[8,4,4096]{2,1,0:T(4,128)(2,1)S(1)} %fusion.35), channel_id=1, source_target_pairs={{0,1},{1,0},{2,3},{3,2},{4,5},{5,4},{6,7},{7,6},{8,9},{9,8},{10,11... | collective-permute-start | bytes 786440 | tf_op jit(solution)/shard_map/ppermute | solution.py:43
  282.7 15.1 %all_to_all.20 = bf16[8,4,4096]{2,1,0:T(4,128)(2,1)S(1)} all-to-all(bf16[8,4,4096]{2,1,0:T(4,128)(2,1)S(1)} %fusion.31), channel_id=1, replica_groups=mesh['z'=12,'x'=4,'y'=8,'core'=2] {'y'}, dimensions={0} | all-to-all | bytes 524288 | tf_op jit(solution)/shard_map/all_to_all | solution.py:45
  (81 shorter events, 23.6 us)
Async XLA Ops:
  0.0 37.1 %collective-permute-start = (bf16[1,4096,128]{2,1,0:T(8,128)(2,1)}, bf16[1,4096,128]{2,1,0:T(8,128)(2,1)S(1)}, u32[]{:S(2)}, u32[]{:S(2)}) collective-permute-start(bf16[1,4096,128]{2,1,0:T(8,128)(2,1)} %refs_1_.1), channel_id=1, source_target_pairs={{0,16},{16,0},{32,48},{48,32},{64,80},{80,64},{96,112},{112,96},{1... | collective-permute-start | bytes 3145736 | tf_op jit(solution)/shard_map/ppermute | solution.py:125
  37.1 24.4 %copy-start.5 = (bf16[1,4096,128]{2,1,0:T(8,128)(2,1)}, bf16[1,4096,128]{2,1,0:T(8,128)(2,1)S(1)}, u32[]{:S(2)}) copy-start(bf16[1,4096,128]{2,1,0:T(8,128)(2,1)S(1)} %collective-permute-done.refs_3_) | copy-start | bytes 3145732
  47.9 13.0 %collective-permute-start.1 = (bf16[3072,128]{1,0:T(8,128)(2,1)S(1)}, bf16[3072,128]{1,0:T(8,128)(2,1)S(1)}, u32[]{:S(2)}, u32[]{:S(2)}) collective-permute-start(bf16[3072,128]{1,0:T(8,128)(2,1)S(1)} %bitcast.57), channel_id=1, source_target_pairs={{0,1},{1,0},{2,3},{3,2},{4,5},{5,4},{6,7},{7,6},{8,9},{9,8},{10,11... | collective-permute-start | bytes 2359304 | tf_op jit(solution)/shard_map/ppermute | solution.py:140
  61.6 1.7 copy-start.9
  67.2 14.4 %copy-start.1 = (bf16[1,4096,128]{2,1,0:T(8,128)(2,1)S(1)}, bf16[1,4096,128]{2,1,0:T(8,128)(2,1)}, u32[]{:S(2)}) copy-start(bf16[1,4096,128]{2,1,0:T(8,128)(2,1)} %refs_2_.1) | copy-start | bytes 3145732
  67.3 16.9 %copy-start.11 = (s32[64,8]{0,1:T(8,128)S(1)}, s32[64,8]{0,1:T(8,128)}, u32[]{:S(2)}) copy-start(s32[64,8]{0,1:T(8,128)} %param.23) | copy-start | bytes 6148
  67.3 17.0 %copy-start.12 = (s32[64,8]{0,1:T(8,128)S(1)}, s32[64,8]{0,1:T(8,128)}, u32[]{:S(2)}) copy-start(s32[64,8]{0,1:T(8,128)} %param.24) | copy-start | bytes 6148
  67.3 40.5 %copy-start.10 = (f32[4096]{0:T(1024)S(1)}, f32[4096]{0:T(1024)}, u32[]{:S(2)}) copy-start(f32[4096]{0:T(1024)} %param.19) | copy-start | bytes 49156
  70.5 3.4 %collective-permute-start.2 = (bf16[8,4,4096]{2,0,1:T(8,128)(2,1)S(1)}, bf16[8,4,4096]{2,0,1:T(8,128)(2,1)S(1)}, u32[]{:S(2)}, u32[]{:S(2)}) collective-permute-start(bf16[8,4,4096]{2,0,1:T(8,128)(2,1)S(1)} %fusion.34), channel_id=1, source_target_pairs={{0,1},{1,0},{2,3},{3,2},{4,5},{5,4},{6,7},{7,6},{8,9},{9,8},{10,11... | collective-permute-start | bytes 786440 | tf_op jit(solution)/shard_map/ppermute | solution.py:43
  74.8 17.9 %all-to-all-start = ((bf16[8,4,4096]{2,1,0:T(4,128)(2,1)}), bf16[8,4,4096]{2,1,0:T(4,128)(2,1)S(1)}, u32[]{:S(2)}, u32[]{:S(2)}) async-start(bf16[8,4,4096]{2,1,0:T(4,128)(2,1)} %copy.43), calls=%async_computation | async-start | bytes 524288 | tf_op jit(solution)/shard_map/all_to_all | solution.py:45
  81.7 25.9 %collective-permute-start.3 = (bf16[1,4096,128]{2,1,0:T(8,128)(2,1)S(1)}, bf16[1,4096,128]{2,1,0:T(8,128)(2,1)S(1)}, u32[]{:S(2)}, u32[]{:S(2)}) collective-permute-start(bf16[1,4096,128]{2,1,0:T(8,128)(2,1)S(1)} %copy-done.1), channel_id=1, source_target_pairs={{0,16},{16,0},{32,48},{48,32},{64,80},{80,64},{96,112},{112,96},{1... | collective-permute-start | bytes 3145736 | tf_op jit(solution)/shard_map/ppermute | solution.py:126
  107.6 20.2 %copy-start.7 = (bf16[1,4096,128]{2,1,0:T(8,128)(2,1)}, bf16[1,4096,128]{2,1,0:T(8,128)(2,1)S(1)}, u32[]{:S(2)}) copy-start(bf16[1,4096,128]{2,1,0:T(8,128)(2,1)S(1)} %collective-permute-done.3.refs_4_) | copy-start | bytes 3145732
  129.6 9.3 %copy-start.3 = (bf16[1,128,4096]{2,1,0:T(8,128)(2,1)S(1)}, bf16[1,128,4096]{2,1,0:T(8,128)(2,1)}, u32[]{:S(2)}) copy-start(bf16[1,128,4096]{2,1,0:T(8,128)(2,1)} %refs_5_.1) | copy-start | bytes 3145732
  133.4 62.2 %all-to-all-start.1 = ((bf16[48,4,4096]{2,1,0:T(4,128)(2,1)}), bf16[48,4,4096]{2,1,0:T(4,128)(2,1)}, u32[]{:S(2)}, u32[]{:S(2)}) async-start(bf16[48,4,4096]{2,1,0:T(4,128)(2,1)} %reshape.376), calls=%async_computation.1 | async-start | bytes 3145728 | tf_op jit(solution)/shard_map/all_to_all | solution.py:192
  139.0 59.0 %collective-permute-start.4 = (bf16[1,128,4096]{2,1,0:T(8,128)(2,1)S(1)}, bf16[1,128,4096]{2,1,0:T(8,128)(2,1)}, u32[]{:S(2)}, u32[]{:S(2)}) collective-permute-start(bf16[1,128,4096]{2,1,0:T(8,128)(2,1)S(1)} %copy-done.3), channel_id=1, source_target_pairs={{0,16},{16,0},{32,48},{48,32},{64,80},{80,64},{96,112},{112,96},{1... | collective-permute-start | bytes 3145736 | tf_op jit(solution)/shard_map/ppermute | solution.py:127
  198.0 1.2 copy-start
  199.2 1.2 copy-start.2
  200.4 1.2 copy-start.4
  201.6 1.2 copy-start.6
  202.9 1.2 copy-start.8
  209.4 9.1 %copy-start.13 = (f32[64,8]{0,1:T(8,128)S(1)}, f32[64,8]{0,1:T(8,128)}, u32[]{:S(2)}) copy-start(f32[64,8]{0,1:T(8,128)} %param.25) | copy-start | bytes 6148
  211.4 61.3 %all-to-all-start.2 = ((bf16[48,4,4096]{2,1,0:T(4,128)(2,1)}), bf16[48,4,4096]{2,1,0:T(4,128)(2,1)S(1)}, u32[]{:S(2)}, u32[]{:S(2)}) async-start(bf16[48,4,4096]{2,1,0:T(4,128)(2,1)} %reshape.378), calls=%async_computation.2 | async-start | bytes 3145728 | tf_op jit(solution)/shard_map/all_to_all | solution.py:202
  274.4 8.1 %collective-permute-start.5 = (bf16[8,4,4096]{2,1,0:T(4,128)(2,1)S(1)}, bf16[8,4,4096]{2,1,0:T(4,128)(2,1)S(1)}, u32[]{:S(2)}, u32[]{:S(2)}) collective-permute-start(bf16[8,4,4096]{2,1,0:T(4,128)(2,1)S(1)} %fusion.35), channel_id=1, source_target_pairs={{0,1},{1,0},{2,3},{3,2},{4,5},{5,4},{6,7},{7,6},{8,9},{9,8},{10,11... | collective-permute-start | bytes 786440 | tf_op jit(solution)/shard_map/ppermute | solution.py:43

commit v3 on v2

v3 whole, which is shorter than its diff:
```python
import jax
import jax.numpy as jnp
import numpy as np
from jax import lax
from jax.experimental import pallas as pl
from jax.experimental.pallas import tpu as pltpu
from jax.sharding import Mesh
from jax.sharding import PartitionSpec as P

QUERY_HEADS = 64
KEY_VALUE_HEADS = 4
EXPERTS = 128
SLICES = 6
CAP = 8
THETA = 1000000.0
CTX = ("z", "xh", "xl")
EXP = ("y", "core")
SWAP = [(0, 1), (1, 0)]


def tables(tokens, head_dim):
    half = head_dim // 2
    inverse = np.float32(THETA) ** (-(np.arange(half, dtype=np.float32) * 2.0 / head_dim))
    angle = np.arange(tokens, dtype=np.float32)[:, None] * inverse.astype(np.float32)[None, :]
    return np.concatenate([np.cos(angle), np.sin(angle)], axis=1).astype(np.float32)


def norm_rotate(rows, gain, table):
    half = rows.shape[-1] // 2
    mean_square = jnp.mean(rows * rows, axis=-1, keepdims=True)
    rows = rows * lax.rsqrt(mean_square + 1e-06) * gain
    first, second = rows[:, :half], rows[:, half:]
    cosine, sine = table[:, :half], table[:, half:]
    return jnp.concatenate(
        [first * cosine - second * sine, second * cosine + first * sine], axis=-1
    )


def prepare_kernel(place_ref, kv_ref, q_ref, key_gain_ref, query_gain_ref, table_ref, mine_ref, query_ref):
    rows, head_dim = mine_ref.shape
    table = table_ref[...]
    keys = norm_rotate(kv_ref[0].astype(jnp.float32), key_gain_ref[...], table)
    mine_ref[...] = jnp.where(place_ref[0] == 0, keys.astype(jnp.bfloat16), kv_ref[1])
    for h in range(q_ref.shape[1] // head_dim):
        head = q_ref[:, h * head_dim : (h + 1) * head_dim].astype(jnp.float32)
        query_ref[h * rows : (h + 1) * rows, :] = norm_rotate(
            head, query_gain_ref[...], table
        ).astype(jnp.bfloat16)


def prepare(place, key_value, queries, key_gain, query_gain, table):
    rows, width = queries.shape
    head_dim = table.shape[1]
    fixed = lambda i, place: (0, 0)
    return pl.pallas_call(
        prepare_kernel,
        grid_spec=pltpu.PrefetchScalarGridSpec(
            num_scalar_prefetch=1,
            grid=(1,),
            in_specs=[
                pl.BlockSpec((2, rows, head_dim), lambda i, place: (0, 0, place[2])),
                pl.BlockSpec((rows, width), fixed),
                pl.BlockSpec((1, head_dim), fixed),
                pl.BlockSpec((1, head_dim), fixed),
                pl.BlockSpec((rows, head_dim), lambda i, place: (place[1], 0)),
            ],
            out_specs=[
                pl.BlockSpec((rows, head_dim), fixed),
                pl.BlockSpec((rows * width // head_dim, head_dim), fixed),
            ],
        ),
        out_shape=[
            jax.ShapeDtypeStruct((rows, head_dim), jnp.bfloat16),
            jax.ShapeDtypeStruct((rows * width // head_dim, head_dim), jnp.bfloat16),
        ],
        compiler_params=pltpu.CompilerParams(vmem_limit_bytes=62 * 1024 * 1024),
    )(place, key_value, queries, key_gain, query_gain, table)


def attention_kernel(chunks, n_x, rows, place_ref, query_ref, mine_ref, other_ref, out_ref, scores):
    total_keys, head_dim = mine_ref.shape
    heads = query_ref.shape[0] // rows
    size = total_keys // chunks
    core, ctx_index = place_ref[0], place_ref[1]
    scale = 1.0 / head_dim**0.5
    query = query_ref[...]
    token = ctx_index * rows + lax.broadcasted_iota(jnp.int32, (rows, size), 0)
    key = lax.broadcasted_iota(jnp.int32, (rows, size), 1)
    key = (key // rows) * (n_x * rows) + key % rows
    peak = None
    for j in range(chunks):
        part = pl.ds(j * size, size)
        keys = jnp.where(core == 0, mine_ref[part, :], other_ref[part, :])
        found = (
            lax.dot_general(
                query, keys, (((1,), (1,)), ((), ())), preferred_element_type=jnp.float32
            )
            * scale
        )
        visible = jnp.concatenate([key + j * rows <= token] * heads, axis=0)
        found = jnp.where(visible, found, -1e30)
        scores[:, part] = found
        top = jnp.max(found, axis=-1, keepdims=True)
        peak = top if peak is None else jnp.maximum(peak, top)
    total = jnp.zeros_like(peak)
    accum = jnp.zeros((heads * rows, head_dim), jnp.float32)
    for j in range(chunks):
        part = pl.ds(j * size, size)
        values = jnp.where(core == 0, other_ref[part, :], mine_ref[part, :])
        weights = jnp.exp(scores[:, part] - peak)
        total += jnp.sum(weights, axis=-1, keepdims=True)
        accum += jnp.dot(
            weights.astype(jnp.bfloat16), values, preferred_element_type=jnp.float32
        )
    attended = (accum / total).astype(jnp.bfloat16)
    attended = jnp.concatenate(
        [attended[h * rows : (h + 1) * rows] for h in range(heads)], axis=1
    )
    place = lax.broadcasted_iota(jnp.int32, (rows, rows), 0)
    keeper = jnp.where(place < rows // 2, 1 - core, core)
    place = place % (rows // 2)
    source = (place // 4) * 8 + keeper * 4 + place % 4
    order = (source == lax.broadcasted_iota(jnp.int32, (rows, rows), 1)).astype(jnp.float32)
    out_ref[...] = jnp.dot(
        order.astype(jnp.bfloat16), attended, preferred_element_type=jnp.float32
    ).astype(jnp.bfloat16)


def attend(place, query, mine, other, rows, n_x):
    count, head_dim = query.shape
    total_keys = mine.shape[0]
    whole = pl.BlockSpec(memory_space=pltpu.VMEM)
    return pl.pallas_call(
        lambda *refs: attention_kernel(n_x, n_x, rows, *refs),
        in_specs=[pl.BlockSpec(memory_space=pltpu.SMEM)] + [whole] * 3,
        out_specs=whole,
        out_shape=jax.ShapeDtypeStruct((rows, count // rows * head_dim), jnp.bfloat16),
        scratch_shapes=[pltpu.VMEM((count, total_keys), jnp.float32)],
        compiler_params=pltpu.CompilerParams(vmem_limit_bytes=20 * 1024 * 1024),
        cost_estimate=pl.CostEstimate(
            flops=4 * count * head_dim * total_keys,
            bytes_accessed=16 * 1024 * 1024,
            transcendentals=count * total_keys,
        ),
    )(place, query, mine, other)


def expert_kernel(chunks, *refs):
    x_ref, ga_ref, ua_ref, gb_ref, ub_ref, da_ref, db_ref, out_ref, x, into, back, out, sems = refs
    width = x.shape[1]
    hidden = back.shape[0] // 2
    depth = width // chunks
    parts = [pl.ds(j * depth, depth) for j in range(chunks)]
    pairs = []
    for part in parts:
        group = [(x_ref.at[:, part], x.at[:, part])]
        for i, ref in enumerate((ga_ref, gb_ref, ua_ref, ub_ref)):
            group.append((ref.at[0, part, :], into.at[part, pl.ds(i * hidden, hidden)]))
        pairs.append(group)
    pairs.append(
        [
            (ref.at[0], back.at[pl.ds(i * hidden, hidden), :])
            for i, ref in enumerate((da_ref, db_ref))
        ]
    )
    copies = [
        [
            pltpu.make_async_copy(source, target, sems.at[j * 5 + i])
            for i, (source, target) in enumerate(group)
        ]
        for j, group in enumerate(pairs)
    ]
    for group in copies:
        for copy in group:
            copy.start()
    sums = None
    for j, part in enumerate(parts):
        for copy in copies[j]:
            copy.wait()
        term = jnp.dot(x[:, part], into[part, :], preferred_element_type=jnp.float32)
        sums = term if sums is None else sums + term
    gate, upper = sums[:, : 2 * hidden], sums[:, 2 * hidden :]
    act = (gate / (1.0 + jnp.exp(-gate)) * upper).astype(jnp.bfloat16)
    for copy in copies[chunks]:
        copy.wait()
    results = []
    for j, part in enumerate(parts):
        out[:, part] = jnp.dot(act, back[:, part], preferred_element_type=jnp.float32).astype(
            jnp.bfloat16
        )
        results.append(
            pltpu.make_async_copy(out.at[:, part], out_ref.at[:, part], sems.at[chunks * 5 + 2 + j])
        )
        results[-1].start()
    for copy in results:
        copy.wait()


def expert_pair(rows, gate_a, up_a, gate_b, up_b, down_a, down_b):
    count, width = rows.shape
    hidden = gate_a.shape[-1]
    chunks = 4
    anywhere = pl.BlockSpec(memory_space=pl.ANY)
    return pl.pallas_call(
        lambda *refs: expert_kernel(chunks, *refs),
        in_specs=[anywhere] * 7,
        out_specs=anywhere,
        out_shape=jax.ShapeDtypeStruct((count, width), jnp.bfloat16),
        scratch_shapes=[
            pltpu.VMEM((count, width), jnp.bfloat16),
            pltpu.VMEM((width, 4 * hidden), jnp.bfloat16),
            pltpu.VMEM((2 * hidden, width), jnp.bfloat16),
            pltpu.VMEM((count, width), jnp.bfloat16),
            pltpu.SemaphoreType.DMA((chunks * 6 + 2,)),
        ],
        compiler_params=pltpu.CompilerParams(vmem_limit_bytes=60 * 1024 * 1024),
        cost_estimate=pl.CostEstimate(
            flops=12 * count * width * hidden,
            bytes_accessed=4 * count * width + 12 * width * hidden,
            transcendentals=2 * count * hidden,
        ),
    )(rows, gate_a, up_a, gate_b, up_b, down_a, down_b)


def shares_over_exp(give, keep):
    n_y = lax.axis_size("y")
    got = lax.ppermute(give.astype(jnp.bfloat16), "core", SWAP)
    both = (keep + got.astype(jnp.float32)).astype(jnp.bfloat16)
    both = both.reshape(n_y, both.shape[0] // n_y, -1)
    return lax.all_to_all(both, "y", split_axis=0, concat_axis=0, tiled=True)


def add_terms(ref):
    total = ref[0].astype(jnp.float32)
    for i in range(1, ref.shape[0]):
        total += ref[i].astype(jnp.float32)
    return total


def stream_kernel(terms_ref, residual_ref, gain_ref, stream_ref, normed_ref):
    stream = residual_ref[...].astype(jnp.float32) + add_terms(terms_ref)
    mean_square = jnp.mean(stream * stream, axis=-1, keepdims=True)
    stream_ref[...] = stream
    normed_ref[...] = (stream * lax.rsqrt(mean_square + 1e-06) * gain_ref[...]).astype(
        jnp.bfloat16
    )


def finish_kernel(terms_ref, stream_ref, out_ref):
    out_ref[...] = (stream_ref[...] + add_terms(terms_ref)).astype(jnp.bfloat16)


def on_vmem(kernel, out_shape, *arguments):
    whole = pl.BlockSpec(memory_space=pltpu.VMEM)
    return pl.pallas_call(
        kernel,
        in_specs=[whole] * len(arguments),
        out_specs=jax.tree.map(lambda _: whole, out_shape),
        out_shape=out_shape,
        compiler_params=pltpu.CompilerParams(vmem_limit_bytes=4 * 1024 * 1024),
    )(*arguments)


def body(
    residual_in,
    queries,
    projected_key_value,
    query_gain,
    key_norm_gain,
    output_weight,
    norm_gain,
    gate_weight,
    up_weight,
    down_weight,
    expert_index,
    expert_slot,
    route_weight,
):
    rows = queries.shape[0]
    head_dim = query_gain.shape[0]
    local_heads = queries.shape[1] // head_dim
    n_x = lax.axis_size("xh") * lax.axis_size("xl")
    n_z = lax.axis_size("z")
    n_ctx = n_x * n_z
    n_exp = lax.axis_size("y") * lax.axis_size("core")
    core = lax.axis_index("core")
    ctx_index = lax.axis_index("z") * n_x + lax.axis_index("xh") * 2 + lax.axis_index("xl")
    exp_index = lax.axis_index("y") * 2 + core
    key_value_head = exp_index * local_heads // (QUERY_HEADS // KEY_VALUE_HEADS)
    place = jnp.stack([core, ctx_index, key_value_head]).astype(jnp.int32)
    table = jnp.asarray(tables(n_ctx * rows, head_dim))

    gate_other = lax.ppermute(gate_weight, "xl", SWAP)
    up_other = lax.ppermute(up_weight, "xl", SWAP)
    down_other = lax.ppermute(down_weight, "xl", SWAP)

    mine, query = prepare(
        place,
        projected_key_value,
        queries,
        key_norm_gain[None, :],
        query_gain[None, :],
        table,
    )
    mine = lax.all_gather(mine[None], "z", axis=0, tiled=True)
    mine, gate_other = lax.optimization_barrier((mine, gate_other))
    mine = lax.all_gather(mine[None], ("xh", "xl"), axis=0, tiled=True)
    mine = mine.reshape(n_ctx * rows, head_dim)
    other = lax.ppermute(mine, "core", SWAP)
    attended = attend(place, query, mine, other, rows, n_x)
    product = jnp.dot(attended, output_weight, preferred_element_type=jnp.float32)
    give, keep = product[: rows // 2], product[rows // 2 :]
    share = rows // n_exp
    own_residual = lax.dynamic_slice_in_dim(residual_in, exp_index * share, share, 0)
    width = own_residual.shape[-1]
    own_stream, own_normed = on_vmem(
        stream_kernel,
        [
            jax.ShapeDtypeStruct((share, width), jnp.float32),
            jax.ShapeDtypeStruct((share, width), jnp.bfloat16),
        ],
        shares_over_exp(give, keep),
        own_residual,
        norm_gain[None, :],
    )
    normed = lax.all_gather(own_normed, EXP, axis=0, tiled=True)
    normed, up_other = lax.optimization_barrier((normed, up_other))

    local = EXPERTS // n_exp
    pairs = SLICES // 2
    peers = local * pairs
    lanes = peers * CAP
    lane = jnp.arange(lanes, dtype=jnp.int32)
    lane_expert = lane // (pairs * CAP) + exp_index * local
    lane_slot = lane % CAP
    match = (expert_index[:, :, None] == lane_expert) & (expert_slot[:, :, None] == lane_slot)
    select = jnp.any(match, axis=1).astype(jnp.bfloat16)
    combine = jnp.sum(jnp.where(match, route_weight[:, :, None], 0.0), axis=1)
    combine = combine.reshape(n_exp // 2, 2, share, lanes)
    combine = jnp.concatenate(
        [lax.dynamic_index_in_dim(combine, i, 1, False) for i in (1 - core, core)], axis=0
    ).reshape(rows, lanes)
    combine_high = combine.astype(jnp.bfloat16)
    combine_low = (combine - combine_high.astype(jnp.float32)).astype(jnp.bfloat16)
    combine = jnp.concatenate([combine_high, combine_low], axis=0)

    outgoing = lax.dot_general(
        select, normed, (((0,), (0,)), ((), ())), preferred_element_type=jnp.float32
    ).astype(jnp.bfloat16)
    outgoing = outgoing.reshape(peers, CAP, width)
    arrived = lax.all_to_all(outgoing, ("z", "xh"), split_axis=0, concat_axis=0, tiled=True)
    pieces = expert_pair(
        arrived.reshape(lanes, width),
        gate_weight,
        up_weight,
        gate_other,
        up_other,
        down_weight,
        down_other,
    ).reshape(peers, CAP, width)
    returned = lax.all_to_all(pieces, ("z", "xh"), split_axis=0, concat_axis=0, tiled=True)
    returned = returned.reshape(lanes, width)
    mixture = jnp.dot(combine, returned, preferred_element_type=jnp.float32)
    mixture = mixture[:rows] + mixture[rows:]
    return on_vmem(
        finish_kernel,
        jax.ShapeDtypeStruct((share, width), jnp.bfloat16),
        shares_over_exp(mixture[: rows // 2], mixture[rows // 2 :]),
        own_stream,
    )


def solution(mesh):
    shape = (12, 2, 2, 8, 2)
    fine = Mesh(np.asarray(mesh.devices).reshape(shape), CTX + EXP)
    in_specs = (
        P(CTX, None),
        P(CTX, EXP),
        P(None, CTX, None),
        P(),
        P(),
        P(EXP, None),
        P(),
        P(EXP + CTX, None, None),
        P(EXP + CTX, None, None),
        P(EXP + CTX, None, None),
        P(CTX, None),
        P(CTX, None),
        P(CTX, None),
    )
    out_specs = P(CTX + EXP, None)
    return jax.shard_map(body, mesh=fine, in_specs=in_specs, out_specs=out_specs, check_vma=False)
```

time: 300 us -> 264 us (0.88)
  local copies, waits for them, and re-layouts: 18.1 us -> 3.45 us
  waiting for transfers between devices: 134 us -> 125 us
  other arithmetic: 8.19 us -> 1.48 us
  Pallas kernels: 5.3 us -> 10.9 us
  starting transfers between devices: 49.2 us -> 44.1 us
  matrix products: 10.2 us -> 6.72 us
    all_to_all x3, waiting for transfers between devices: 116 us -> 90.4 us  [the longest x1 56.6 us: body(): lax.all_to_all(pieces, ('z', 'xh'), split_axis=0, concat_axis=0, tiled=True)]
    ppermute x6, waiting for transfers between devices: 17.9 us -> 35 us  [the longest x1 31.9 us: body(): down_other = lax.ppermute(down_weight, 'xl', SWAP)]
    reshape x5 -> x4, local copies, waits for them, and re-layouts: 8.79 us -> 0.95 us  [the longest x2 0.91 us: shares_over_exp(): both = both.reshape(n_y, both.shape[0] // n_y, -1)]
    pallas_call x1 -> x5, Pallas kernels: 5.3 us -> 10.9 us  [the longest x1 4.95 us: expert_pair(): pl.pallas_call(lambda *refs: expert_kernel(chunks, *refs), in_specs=[anyw...]
    unnamed x32 -> x25, local copies, waits for them, and re-layouts: 7.12 us -> 2.28 us
    ppermute x6, starting transfers between devices: 29.7 us -> 25.3 us  [the longest x1 11.4 us: body(): other = lax.ppermute(mine, 'core', SWAP)]
    dot_general x4 -> x1, matrix products: 5.35 us -> 1.84 us  [body(): mixture = jnp.dot(combine, returned, preferred_element_type=jnp.float32)]
  transfers between devices with their start and end apart: 9 -> 9, of which waited for: 7 -> 6; matrix products, arithmetic and copies ran while one was open for 3% -> 1% of each run, Pallas kernels for 0% -> 1%
where the time goes in v3:
time: 264 us; the launch traced here: 263 us
  waiting for transfers between devices  125 us (47%)
  blocking collectives  70.7 us (27%)
  starting transfers between devices  44.1 us (17%)
  Pallas kernels  10.9 us (4%)
  matrix products  6.72 us (3%)
  local copies, waits for them, and re-layouts  3.45 us (1%)
    all_to_all x1, waiting for transfers between devices, body(): lax.all_to_all(pieces, ('z', 'xh'), split_axis=0, concat_axis=0, tiled=True)  56.6 us
    ppermute x1, waiting for transfers between devices, body(): down_other = lax.ppermute(down_weight, 'xl', SWAP)  31.9 us
    all_gather x1, blocking collectives, body(): mine = lax.all_gather(mine[None], 'z', axis=0, tiled=True)  28 us
    all_to_all x1, waiting for transfers between devices, body(): lax.all_to_all(outgoing, ('z', 'xh'), split_axis=0, concat_axis=0, tiled=...  23.3 us
    all_gather x1, blocking collectives, body(): normed = lax.all_gather(own_normed, EXP, axis=0, tiled=True)  18 us
    all_to_all x1, blocking collectives, shares_over_exp(): return lax.all_to_all(both, 'y', split_axis=0, concat_axis=0, tiled=True)  14.2 us
    ppermute x1, starting transfers between devices, body(): other = lax.ppermute(mine, 'core', SWAP)  11.4 us
    all_to_all x1, waiting for transfers between devices, shares_over_exp(): return lax.all_to_all(both, 'y', split_axis=0, concat_axis=0, tiled=True)  10.5 us
  transfers between devices with their start and end apart: 9, of which 6 were waited for; matrix products, arithmetic and copies ran while one was open for 1% of the time, Pallas kernels for 1%

profile of v3, /device:TPU:1, one launch (start us, length us, event | category | flops | bytes accessed | tf_op | source)
XLA Modules:
  0.0 263.1 jit_solution(2501797738493833879)
XLA Ops:
  0.0 4.1 %collective-permute-start = (bf16[1,4096,128]{2,1,0:T(8,128)(2,1)}, bf16[1,4096,128]{2,1,0:T(8,128)(2,1)S(1)}, u32[]{:S(2)}, u32[]{:S(2)}) collective-permute-start(bf16[1,4096,128]{2,1,0:T(8,128)(2,1)} %refs_1_.1), channel_id=1, source_target_pairs={{0,16},{16,0},{1,17},{17,1},{2,18},{18,2},{3,19},{19,3},{4,20},{20... | collective-permute-start | bytes 3145736 | tf_op jit(solution)/shard_map/ppermute | solution.py:293
  4.8 2.7 %shard_map.136 = (bf16[64,128]{1,0:T(8,128)(2,1)}, bf16[256,128]{1,0:T(8,128)(2,1)}) custom-call(s32[3]{0:T(128)} %pad_add_fusion.place_ref.refs_0_, bf16[2,64,512]{2,1,0:T(8,128)(2,1)} %kv_ref.1, bf16[64,512]{1,0:T(8,128)(2,1)} %q_ref.1, f32[1,128]{1,0:T(1,128)} %bitcast.31, f32[1,128]{1,0:T(1,128)} %bitcast.32, f32[3072,128]{1,0:T(8,128)} %constant.81.clone.table_ref), custom_call_target="tpu_custom_call" | custom-call | tf_op jit(solution)/shard_map/pallas_call | solution.py:55
  7.5 28.0 %all-gather = bf16[768,128]{1,0:T(8,128)(2,1)S(1)} all-gather(bf16[64,128]{1,0:T(8,128)(2,1)} %get-tuple-element.14), channel_id=2, replica_groups=mesh['z'=12,'xh'=2,'xl'=2,'y'=8,'core'=2] {'z'}, dimensions={0}, use_global_device_ids=true | all-gather | bytes 212992 | tf_op jit(solution)/shard_map/all_gather | solution.py:305
  35.6 10.5 %all-gather.1 = bf16[48,64,128]{2,1,0:T(8,128)(2,1)S(1)} all-gather(bf16[12,64,128]{2,1,0:T(8,128)(2,1)S(1)} %bitcast.30), channel_id=3, replica_groups=mesh['z'=12,'xh'=2,'xl'=2,'y'=8,'core'=2] {'xh','xl'}, dimensions={0}, use_global_device_ids=true | all-gather | bytes 983040 | tf_op jit(solution)/shard_map/all_gather | solution.py:307
  46.0 11.4 %collective-permute-start.1 = (bf16[3072,128]{1,0:T(8,128)(2,1)S(1)}, bf16[3072,128]{1,0:T(8,128)(2,1)S(1)}, u32[]{:S(2)}, u32[]{:S(2)}) collective-permute-start(bf16[3072,128]{1,0:T(8,128)(2,1)S(1)} %bitcast.24), channel_id=1, source_target_pairs={{0,1},{1,0},{2,3},{3,2},{4,5},{5,4},{6,7},{7,6},{8,9},{9,8},{10,11... | collective-permute-start | bytes 2359304 | tf_op jit(solution)/shard_map/ppermute | solution.py:309
  57.4 1.9 collective-permute-done.1.refs_3_
  60.1 2.4 shard_map.137
  62.6 3.1 %fusion.11 = f32[64,4096]{1,0:T(8,128)S(1)} fusion(bf16[64,512]{1,0:T(8,128)(2,1)S(1)} %shard_map.137, bf16[512,4096]{1,0:T(8,128)(2,1)} %param.19), kind=kOutput, calls=%fused_computation.30 | convolution fusion | flops 268435456 | bytes 5308416 | tf_op jit(solution)/shard_map/dot_general | solution.py:311
  65.8 2.3 collective-permute-start.2
  68.1 2.5 collective-permute-start.3
  71.6 6.8 %all-to-all-start = ((bf16[8,4,4096]{2,1,0:T(4,128)(2,1)}), bf16[8,4,4096]{2,1,0:T(4,128)(2,1)S(1)}, u32[]{:S(2)}, u32[]{:S(2)}) async-start(bf16[8,4,4096]{2,1,0:T(4,128)(2,1)} %reshape.56), calls=%async_computation | async-start | bytes 524288 | tf_op jit(solution)/shard_map/all_to_all | solution.py:230
  78.7 10.5 %all-to-all-done.terms_ref = bf16[8,4,4096]{2,1,0:T(4,128)(2,1)S(1)} async-done(((bf16[8,4,4096]{2,1,0:T(4,128)(2,1)}), bf16[8,4,4096]{2,1,0:T(4,128)(2,1)S(1)}, u32[]{:S(2)}, u32[]{:S(2)}) %all-to-all-start) | async-done | bytes 262176 | tf_op jit(solution)/shard_map/all_to_all | solution.py:230
  89.4 18.0 %all-gather.2 = bf16[16,4,4096]{2,1,0:T(4,128)(2,1)S(1)} all-gather(bf16[1,4,4096]{2,1,0:T(4,128)(2,1)S(1)} %bitcast.26), channel_id=1, replica_groups=mesh['z'=12,'xh'=2,'xl'=2,'y'=8,'core'=2] {'y','core'}, dimensions={0}, use_global_device_ids=true | all-gather | bytes 557056 | tf_op jit(solution)/shard_map/all_gather | solution.py:326
  107.5 1.8 fusion
  109.3 5.3 %all-to-all-start.1 = ((bf16[24,8,4096]{2,1,0:T(8,128)(2,1)}), bf16[24,8,4096]{2,1,0:T(8,128)(2,1)S(1)}, u32[]{:S(2)}, u32[]{:S(2)}) async-start(bf16[24,8,4096]{2,1,0:T(8,128)(2,1)} %fusion), calls=%async_computation.1 | async-start | bytes 3145728 | tf_op jit(solution)/shard_map/all_to_all | solution.py:351
  114.6 1.9 collective-permute-start.4
  116.5 31.9 %collective-permute-done.4.refs_6_ = bf16[1,128,4096]{2,1,0:T(8,128)(2,1)} collective-permute-done((bf16[1,128,4096]{2,1,0:T(8,128)(2,1)S(1)}, bf16[1,128,4096]{2,1,0:T(8,128)(2,1)}, u32[]{:S(2)}, u32[]{:S(2)}) %collective-permute-start.4) | collective-permute-done | bytes 1048608 | tf_op jit(solution)/shard_map/ppermute | solution.py:295
  148.5 23.3 %all-to-all-done.1 = bf16[24,8,4096]{2,1,0:T(8,128)(2,1)S(1)} async-done(((bf16[24,8,4096]{2,1,0:T(8,128)(2,1)}), bf16[24,8,4096]{2,1,0:T(8,128)(2,1)S(1)}, u32[]{:S(2)}, u32[]{:S(2)}) %all-to-all-start.1) | async-done | bytes 1572896 | tf_op jit(solution)/shard_map/all_to_all | solution.py:351
  173.0 4.9 %shard_map.139 = bf16[192,4096]{1,0:T(8,128)(2,1)} custom-call(bf16[192,4096]{1,0:T(8,128)(2,1)} %bitcast.29, bf16[1,4096,128]{2,1,0:T(8,128)(2,1)} %refs_1_.1, bf16[1,4096,128]{2,1,0:T(8,128)(2,1)} %refs_2_.1, bf16[1,4096,128]{2,1,0:T(8,128)(2,1)} %copy-done.7, bf16[1,4096,128]{2,1,0:T(8,128)(2,1)} %collective-permute-done.3.refs_4_, ...), custom_call_target="tpu_custom_call" | custom-call | flops 1207959552 | bytes 9437184 | tf_op jit(solution)/shard_map/pallas_call | solution.py:204
  177.9 6.7 %all-to-all-start.2 = ((bf16[24,8,4096]{2,1,0:T(8,128)(2,1)}), bf16[24,8,4096]{2,1,0:T(8,128)(2,1)}, u32[]{:S(2)}, u32[]{:S(2)}) async-start(bf16[24,8,4096]{2,1,0:T(8,128)(2,1)} %bitcast.28), calls=%async_computation.2 | async-start | bytes 3145728 | tf_op jit(solution)/shard_map/all_to_all | solution.py:361
  185.1 56.6 %all-to-all-done.2 = bf16[24,8,4096]{2,1,0:T(8,128)(2,1)} async-done(((bf16[24,8,4096]{2,1,0:T(8,128)(2,1)}), bf16[24,8,4096]{2,1,0:T(8,128)(2,1)}, u32[]{:S(2)}, u32[]{:S(2)}) %all-to-all-start.2) | async-done | bytes 1572896 | tf_op jit(solution)/shard_map/all_to_all | solution.py:361
  241.7 1.8 fusion.1
  243.7 3.2 %collective-permute-start.5 = (bf16[32,4096]{1,0:T(8,128)(2,1)S(1)}, bf16[32,4096]{1,0:T(8,128)(2,1)S(1)}, u32[]{:S(2)}, u32[]{:S(2)}) collective-permute-start(bf16[32,4096]{1,0:T(8,128)(2,1)S(1)} %slice.42), channel_id=1, source_target_pairs={{0,1},{1,0},{2,3},{3,2},{4,5},{5,4},{6,7},{7,6},{8,9},{9,8},{10,11... | collective-permute-start | bytes 786440 | tf_op jit(solution)/shard_map/ppermute | solution.py:227
  248.2 14.2 %all_to_all.20.terms_ref = bf16[8,4,4096]{2,1,0:T(4,128)(2,1)S(1)} all-to-all(bf16[8,4,4096]{2,1,0:T(4,128)(2,1)S(1)} %reshape.61), channel_id=1, replica_groups=mesh['z'=12,'xh'=2,'xl'=2,'y'=8,'core'=2] {'y'}, dimensions={0} | all-to-all | bytes 524288 | tf_op jit(solution)/shard_map/all_to_all | solution.py:230
  (49 shorter events, 6.9 us)
Async XLA Ops:
  0.0 78.7 %copy-start = (bf16[64,4096]{1,0:T(8,128)(2,1)S(1)}, bf16[64,4096]{1,0:T(8,128)(2,1)}, u32[]{:S(2)}) copy-start(bf16[64,4096]{1,0:T(8,128)(2,1)} %param.14) | copy-start | bytes 1572868
  0.0 35.6 %collective-permute-start = (bf16[1,4096,128]{2,1,0:T(8,128)(2,1)}, bf16[1,4096,128]{2,1,0:T(8,128)(2,1)S(1)}, u32[]{:S(2)}, u32[]{:S(2)}) collective-permute-start(bf16[1,4096,128]{2,1,0:T(8,128)(2,1)} %refs_1_.1), channel_id=1, source_target_pairs={{0,16},{16,0},{1,17},{17,1},{2,18},{18,2},{3,19},{19,3},{4,20},{20... | collective-permute-start | bytes 3145736 | tf_op jit(solution)/shard_map/ppermute | solution.py:293
  4.8 54.5 %copy-start.3 = (s32[3]{0:T(128)S(1)}, s32[3]{0:T(128)}, u32[]{:S(2)}) copy-start(s32[3]{0:T(128)} %pad_add_fusion.place_ref.refs_0_) | copy-start | bytes 40
  35.6 23.7 %copy-start.7 = (bf16[1,4096,128]{2,1,0:T(8,128)(2,1)}, bf16[1,4096,128]{2,1,0:T(8,128)(2,1)S(1)}, u32[]{:S(2)}) copy-start(bf16[1,4096,128]{2,1,0:T(8,128)(2,1)S(1)} %collective-permute-done.refs_3_) | copy-start | bytes 3145732
  46.0 13.3 %collective-permute-start.1 = (bf16[3072,128]{1,0:T(8,128)(2,1)S(1)}, bf16[3072,128]{1,0:T(8,128)(2,1)S(1)}, u32[]{:S(2)}, u32[]{:S(2)}) collective-permute-start(bf16[3072,128]{1,0:T(8,128)(2,1)S(1)} %bitcast.24), channel_id=1, source_target_pairs={{0,1},{1,0},{2,3},{3,2},{4,5},{5,4},{6,7},{7,6},{8,9},{9,8},{10,11... | collective-permute-start | bytes 2359304 | tf_op jit(solution)/shard_map/ppermute | solution.py:309
  59.3 0.8 copy-start.1
  62.6 5.5 %copy-start.5 = (bf16[1,4096,128]{2,1,0:T(8,128)(2,1)S(1)}, bf16[1,4096,128]{2,1,0:T(8,128)(2,1)}, u32[]{:S(2)}) copy-start(bf16[1,4096,128]{2,1,0:T(8,128)(2,1)} %refs_2_.1) | copy-start | bytes 3145732
  62.6 8.0 %copy-start.8 = (s32[64,8]{0,1:T(8,128)S(1)}, s32[64,8]{0,1:T(8,128)}, u32[]{:S(2)}) copy-start(s32[64,8]{0,1:T(8,128)} %param.24) | copy-start | bytes 6148
  62.6 8.0 %copy-start.9 = (s32[64,8]{0,1:T(8,128)S(1)}, s32[64,8]{0,1:T(8,128)}, u32[]{:S(2)}) copy-start(s32[64,8]{0,1:T(8,128)} %param.25) | copy-start | bytes 6148
  65.7 23.5 %copy-start.2 = (f32[4096]{0:T(1024)S(1)}, f32[4096]{0:T(1024)}, u32[]{:S(2)}) copy-start(f32[4096]{0:T(1024)} %param.20) | copy-start | bytes 49156
  65.8 5.0 %collective-permute-start.2 = (bf16[32,4096]{1,0:T(8,128)(2,1)S(1)}, bf16[32,4096]{1,0:T(8,128)(2,1)S(1)}, u32[]{:S(2)}, u32[]{:S(2)}) collective-permute-start(bf16[32,4096]{1,0:T(8,128)(2,1)S(1)} %slice.43), channel_id=1, source_target_pairs={{0,1},{1,0},{2,3},{3,2},{4,5},{5,4},{6,7},{7,6},{8,9},{9,8},{10,11... | collective-permute-start | bytes 786440 | tf_op jit(solution)/shard_map/ppermute | solution.py:227
  68.1 39.4 %collective-permute-start.3 = (bf16[1,4096,128]{2,1,0:T(8,128)(2,1)S(1)}, bf16[1,4096,128]{2,1,0:T(8,128)(2,1)}, u32[]{:S(2)}, u32[]{:S(2)}) collective-permute-start(bf16[1,4096,128]{2,1,0:T(8,128)(2,1)S(1)} %copy-done.5), channel_id=1, source_target_pairs={{0,16},{16,0},{1,17},{17,1},{2,18},{18,2},{3,19},{19,3},{4,20},{20... | collective-permute-start | bytes 3145736 | tf_op jit(solution)/shard_map/ppermute | solution.py:294
  71.6 17.6 %all-to-all-start = ((bf16[8,4,4096]{2,1,0:T(4,128)(2,1)}), bf16[8,4,4096]{2,1,0:T(4,128)(2,1)S(1)}, u32[]{:S(2)}, u32[]{:S(2)}) async-start(bf16[8,4,4096]{2,1,0:T(4,128)(2,1)} %reshape.56), calls=%async_computation | async-start | bytes 524288 | tf_op jit(solution)/shard_map/all_to_all | solution.py:230
  109.3 5.3 %copy-start.6 = (bf16[1,128,4096]{2,1,0:T(8,128)(2,1)S(1)}, bf16[1,128,4096]{2,1,0:T(8,128)(2,1)}, u32[]{:S(2)}) copy-start(bf16[1,128,4096]{2,1,0:T(8,128)(2,1)} %refs_5_.1) | copy-start | bytes 3145732
  109.3 62.5 %all-to-all-start.1 = ((bf16[24,8,4096]{2,1,0:T(8,128)(2,1)}), bf16[24,8,4096]{2,1,0:T(8,128)(2,1)S(1)}, u32[]{:S(2)}, u32[]{:S(2)}) async-start(bf16[24,8,4096]{2,1,0:T(8,128)(2,1)} %fusion), calls=%async_computation.1 | async-start | bytes 3145728 | tf_op jit(solution)/shard_map/all_to_all | solution.py:351
  114.6 33.9 %collective-permute-start.4 = (bf16[1,128,4096]{2,1,0:T(8,128)(2,1)S(1)}, bf16[1,128,4096]{2,1,0:T(8,128)(2,1)}, u32[]{:S(2)}, u32[]{:S(2)}) collective-permute-start(bf16[1,128,4096]{2,1,0:T(8,128)(2,1)S(1)} %copy-done.6), channel_id=1, source_target_pairs={{0,16},{16,0},{1,17},{17,1},{2,18},{18,2},{3,19},{19,3},{4,20},{20... | collective-permute-start | bytes 3145736 | tf_op jit(solution)/shard_map/ppermute | solution.py:295
  171.8 1.1 copy-start.4
  177.9 6.7 %copy-start.10 = (f32[64,8]{0,1:T(8,128)S(1)}, f32[64,8]{0,1:T(8,128)}, u32[]{:S(2)}) copy-start(f32[64,8]{0,1:T(8,128)} %param.26) | copy-start | bytes 6148
  177.9 63.8 %all-to-all-start.2 = ((bf16[24,8,4096]{2,1,0:T(8,128)(2,1)}), bf16[24,8,4096]{2,1,0:T(8,128)(2,1)}, u32[]{:S(2)}, u32[]{:S(2)}) async-start(bf16[24,8,4096]{2,1,0:T(8,128)(2,1)} %bitcast.28), calls=%async_computation.2 | async-start | bytes 3145728 | tf_op jit(solution)/shard_map/all_to_all | solution.py:361
  243.7 4.3 %collective-permute-start.5 = (bf16[32,4096]{1,0:T(8,128)(2,1)S(1)}, bf16[32,4096]{1,0:T(8,128)(2,1)S(1)}, u32[]{:S(2)}, u32[]{:S(2)}) collective-permute-start(bf16[32,4096]{1,0:T(8,128)(2,1)S(1)} %slice.42), channel_id=1, source_target_pairs={{0,1},{1,0},{2,3},{3,2},{4,5},{5,4},{6,7},{7,6},{8,9},{9,8},{10,11... | collective-permute-start | bytes 786440 | tf_op jit(solution)/shard_map/ppermute | solution.py:227

commit v4 on v3

--- a/solution.py
+++ b/solution.py
@@ -73,7 +73,7 @@
             jax.ShapeDtypeStruct((rows, head_dim), jnp.bfloat16),
             jax.ShapeDtypeStruct((rows * width // head_dim, head_dim), jnp.bfloat16),
         ],
-        compiler_params=pltpu.CompilerParams(vmem_limit_bytes=62 * 1024 * 1024),
+        compiler_params=pltpu.CompilerParams(vmem_limit_bytes=59 * 1024 * 1024),
     )(place, key_value, queries, key_gain, query_gain, table)
 
 
@@ -222,12 +222,15 @@
     )(rows, gate_a, up_a, gate_b, up_b, down_a, down_b)
 
 
-def shares_over_exp(give, keep):
+def sum_over_cores(give, keep):
     n_y = lax.axis_size("y")
     got = lax.ppermute(give.astype(jnp.bfloat16), "core", SWAP)
     both = (keep + got.astype(jnp.float32)).astype(jnp.bfloat16)
-    both = both.reshape(n_y, both.shape[0] // n_y, -1)
-    return lax.all_to_all(both, "y", split_axis=0, concat_axis=0, tiled=True)
+    return both.reshape(n_y, both.shape[0] // n_y, -1)
+
+
+def to_owners(blocks):
+    return lax.all_to_all(blocks, "y", split_axis=0, concat_axis=0, tiled=True)
 
 
 def add_terms(ref):
@@ -310,22 +313,6 @@
     attended = attend(place, query, mine, other, rows, n_x)
     product = jnp.dot(attended, output_weight, preferred_element_type=jnp.float32)
     give, keep = product[: rows // 2], product[rows // 2 :]
-    share = rows // n_exp
-    own_residual = lax.dynamic_slice_in_dim(residual_in, exp_index * share, share, 0)
-    width = own_residual.shape[-1]
-    own_stream, own_normed = on_vmem(
-        stream_kernel,
-        [
-            jax.ShapeDtypeStruct((share, width), jnp.float32),
-            jax.ShapeDtypeStruct((share, width), jnp.bfloat16),
-        ],
-        shares_over_exp(give, keep),
-        own_residual,
-        norm_gain[None, :],
-    )
-    normed = lax.all_gather(own_normed, EXP, axis=0, tiled=True)
-    normed, up_other = lax.optimization_barrier((normed, up_other))
-
     local = EXPERTS // n_exp
     pairs = SLICES // 2
     peers = local * pairs
@@ -335,6 +322,24 @@
     lane_slot = lane % CAP
     match = (expert_index[:, :, None] == lane_expert) & (expert_slot[:, :, None] == lane_slot)
     select = jnp.any(match, axis=1).astype(jnp.bfloat16)
+    share = rows // n_exp
+    own_residual = lax.dynamic_slice_in_dim(residual_in, exp_index * share, share, 0)
+    both = sum_over_cores(give, keep)
+    both, own_residual, select = lax.optimization_barrier((both, own_residual, select))
+    width = own_residual.shape[-1]
+    own_stream, own_normed = on_vmem(
+        stream_kernel,
+        [
+            jax.ShapeDtypeStruct((share, width), jnp.float32),
+            jax.ShapeDtypeStruct((share, width), jnp.bfloat16),
+        ],
+        to_owners(both),
+        own_residual,
+        norm_gain[None, :],
+    )
+    normed = lax.all_gather(own_normed, EXP, axis=0, tiled=True)
+    normed, up_other = lax.optimization_barrier((normed, up_other))
+
     combine = jnp.sum(jnp.where(match, route_weight[:, :, None], 0.0), axis=1)
     combine = combine.reshape(n_exp // 2, 2, share, lanes)
     combine = jnp.concatenate(
@@ -365,7 +370,7 @@
     return on_vmem(
         finish_kernel,
         jax.ShapeDtypeStruct((share, width), jnp.bfloat16),
-        shares_over_exp(mixture[: rows // 2], mixture[rows // 2 :]),
+        to_owners(sum_over_cores(mixture[: rows // 2], mixture[rows // 2 :])),
         own_stream,
     )
 

time: 264 us -> 262 us (level)
  blocking collectives: 70.7 us -> 88.4 us
  waiting for transfers between devices: 125 us -> 114 us
  starting transfers between devices: 44.1 us -> 36.9 us
    all_to_all x1 -> x2, blocking collectives: 14.2 us -> 32.5 us  [to_owners(): return lax.all_to_all(blocks, 'y', split_axis=0, concat_axis=0, tiled=True)]
    all_to_all x1 -> x0, waiting for transfers between devices: 10.5 us -> none  [shares_over_exp(): return lax.all_to_all(both, 'y', split_axis=0, concat_axis=0, tiled=True)]
    all_to_all x1 -> x0, starting transfers between devices: 6.82 us -> none  [shares_over_exp(): return lax.all_to_all(both, 'y', split_axis=0, concat_axis=0, tiled=True)]
  transfers between devices with their start and end apart: 9 -> 8, of which waited for: 6 -> 5; matrix products, arithmetic and copies ran while one was open for 1% -> 2% of each run, Pallas kernels for 1% -> 2%
where the time goes in v4:
time: 262 us; the launch traced here: 261 us
  waiting for transfers between devices  114 us (44%)
  blocking collectives  88.4 us (34%)
  starting transfers between devices  36.9 us (14%)
  Pallas kernels  11 us (4%)
  matrix products  5.22 us (2%)
  local copies, waits for them, and re-layouts  3.73 us (1%)
    all_to_all x1, waiting for transfers between devices, body(): lax.all_to_all(pieces, ('z', 'xh'), split_axis=0, concat_axis=0, tiled=True)  56.6 us
    all_to_all x2, blocking collectives, to_owners(): return lax.all_to_all(blocks, 'y', split_axis=0, concat_axis=0, tiled=True)  32.5 us
    ppermute x1, waiting for transfers between devices, body(): down_other = lax.ppermute(down_weight, 'xl', SWAP)  32 us
    all_gather x1, blocking collectives, body(): mine = lax.all_gather(mine[None], 'z', axis=0, tiled=True)  28 us
    all_to_all x1, waiting for transfers between devices, body(): lax.all_to_all(outgoing, ('z', 'xh'), split_axis=0, concat_axis=0, tiled=...  23.3 us
    all_gather x1, blocking collectives, body(): normed = lax.all_gather(own_normed, EXP, axis=0, tiled=True)  17.1 us
    ppermute x1, starting transfers between devices, body(): other = lax.ppermute(mine, 'core', SWAP)  11.1 us
    all_gather x1, blocking collectives, body(): mine = lax.all_gather(mine[None], ('xh', 'xl'), axis=0, tiled=True)  10.8 us
  transfers between devices with their start and end apart: 8, of which 5 were waited for; matrix products, arithmetic and copies ran while one was open for 2% of the time, Pallas kernels for 2%

profile of v4, /device:TPU:1, one launch (start us, length us, event | category | flops | bytes accessed | tf_op | source)
XLA Modules:
  0.0 261.1 jit_solution(1549403772679885175)
XLA Ops:
  0.0 4.1 %collective-permute-start = (bf16[1,4096,128]{2,1,0:T(8,128)(2,1)}, bf16[1,4096,128]{2,1,0:T(8,128)(2,1)S(1)}, u32[]{:S(2)}, u32[]{:S(2)}) collective-permute-start(bf16[1,4096,128]{2,1,0:T(8,128)(2,1)} %refs_1_.1), channel_id=1, source_target_pairs={{0,16},{16,0},{1,17},{17,1},{2,18},{18,2},{3,19},{19,3},{4,20},{20... | collective-permute-start | bytes 3145736 | tf_op jit(solution)/shard_map/ppermute | solution.py:296
  4.7 2.7 %shard_map.136 = (bf16[64,128]{1,0:T(8,128)(2,1)}, bf16[256,128]{1,0:T(8,128)(2,1)}) custom-call(s32[3]{0:T(128)} %pad_add_fusion.place_ref.refs_0_, bf16[2,64,512]{2,1,0:T(8,128)(2,1)} %kv_ref.1, bf16[64,512]{1,0:T(8,128)(2,1)} %q_ref.1, f32[1,128]{1,0:T(1,128)} %bitcast.31, f32[1,128]{1,0:T(1,128)} %bitcast.32, f32[3072,128]{1,0:T(8,128)} %constant.81.clone.table_ref), custom_call_target="tpu_custom_call" | custom-call | tf_op jit(solution)/shard_map/pallas_call | solution.py:55
  7.4 28.0 %all-gather = bf16[768,128]{1,0:T(8,128)(2,1)S(1)} all-gather(bf16[64,128]{1,0:T(8,128)(2,1)} %get-tuple-element.17), channel_id=2, replica_groups=mesh['z'=12,'xh'=2,'xl'=2,'y'=8,'core'=2] {'z'}, dimensions={0}, use_global_device_ids=true | all-gather | bytes 212992 | tf_op jit(solution)/shard_map/all_gather | solution.py:308
  36.5 10.8 %all-gather.1 = bf16[48,64,128]{2,1,0:T(8,128)(2,1)S(1)} all-gather(bf16[12,64,128]{2,1,0:T(8,128)(2,1)S(1)} %bitcast.30), channel_id=3, replica_groups=mesh['z'=12,'xh'=2,'xl'=2,'y'=8,'core'=2] {'xh','xl'}, dimensions={0}, use_global_device_ids=true | all-gather | bytes 983040 | tf_op jit(solution)/shard_map/all_gather | solution.py:310
  47.2 11.1 %collective-permute-start.1 = (bf16[3072,128]{1,0:T(8,128)(2,1)S(1)}, bf16[3072,128]{1,0:T(8,128)(2,1)S(1)}, u32[]{:S(2)}, u32[]{:S(2)}) collective-permute-start(bf16[3072,128]{1,0:T(8,128)(2,1)S(1)} %bitcast.24), channel_id=1, source_target_pairs={{0,1},{1,0},{2,3},{3,2},{4,5},{5,4},{6,7},{7,6},{8,9},{9,8},{10,11... | collective-permute-start | bytes 2359304 | tf_op jit(solution)/shard_map/ppermute | solution.py:312
  58.3 2.5 collective-permute-start.3
  62.1 2.5 shard_map.137
  64.6 3.0 %fusion.11 = f32[64,4096]{1,0:T(8,128)S(1)} fusion(bf16[64,512]{1,0:T(8,128)(2,1)S(1)} %shard_map.137, bf16[512,4096]{1,0:T(8,128)(2,1)} %param.19), kind=kOutput, calls=%fused_computation.30 | convolution fusion | flops 268435456 | bytes 5308416 | tf_op jit(solution)/shard_map/dot_general | solution.py:314
  67.7 2.2 collective-permute-start.2
  70.0 1.2 collective-permute-done.2
  71.3 18.3 %all_to_all.20.terms_ref = bf16[8,4,4096]{2,1,0:T(4,128)(2,1)S(1)} all-to-all(bf16[8,4,4096]{2,1,0:T(4,128)(2,1)S(1)} %reshape.56), channel_id=1, replica_groups=mesh['z'=12,'xh'=2,'xl'=2,'y'=8,'core'=2] {'y'}, dimensions={0} | all-to-all | bytes 524288 | tf_op jit(solution)/shard_map/all_to_all | solution.py:233
  89.8 17.1 %all-gather.2 = bf16[16,4,4096]{2,1,0:T(4,128)(2,1)S(1)} all-gather(bf16[1,4,4096]{2,1,0:T(4,128)(2,1)S(1)} %bitcast.26), channel_id=1, replica_groups=mesh['z'=12,'xh'=2,'xl'=2,'y'=8,'core'=2] {'y','core'}, dimensions={0}, use_global_device_ids=true | all-gather | bytes 557056 | tf_op jit(solution)/shard_map/all_gather | solution.py:340
  107.0 1.8 fusion
  108.8 5.4 %all-to-all-start.1 = ((bf16[24,8,4096]{2,1,0:T(8,128)(2,1)}), bf16[24,8,4096]{2,1,0:T(8,128)(2,1)S(1)}, u32[]{:S(2)}, u32[]{:S(2)}) async-start(bf16[24,8,4096]{2,1,0:T(8,128)(2,1)} %fusion), calls=%async_computation.1 | async-start | bytes 3145728 | tf_op jit(solution)/shard_map/all_to_all | solution.py:356
  114.2 1.9 collective-permute-start.4
  116.2 32.0 %collective-permute-done.4.refs_6_ = bf16[1,128,4096]{2,1,0:T(8,128)(2,1)} collective-permute-done((bf16[1,128,4096]{2,1,0:T(8,128)(2,1)S(1)}, bf16[1,128,4096]{2,1,0:T(8,128)(2,1)}, u32[]{:S(2)}, u32[]{:S(2)}) %collective-permute-start.4) | collective-permute-done | bytes 1048608 | tf_op jit(solution)/shard_map/ppermute | solution.py:298
  148.1 23.3 %all-to-all-done.1 = bf16[24,8,4096]{2,1,0:T(8,128)(2,1)S(1)} async-done(((bf16[24,8,4096]{2,1,0:T(8,128)(2,1)}), bf16[24,8,4096]{2,1,0:T(8,128)(2,1)S(1)}, u32[]{:S(2)}, u32[]{:S(2)}) %all-to-all-start.1) | async-done | bytes 1572896 | tf_op jit(solution)/shard_map/all_to_all | solution.py:356
  171.4 1.1 copy-done.4
  172.6 4.9 %shard_map.139 = bf16[192,4096]{1,0:T(8,128)(2,1)} custom-call(bf16[192,4096]{1,0:T(8,128)(2,1)} %bitcast.29, bf16[1,4096,128]{2,1,0:T(8,128)(2,1)} %refs_1_.1, bf16[1,4096,128]{2,1,0:T(8,128)(2,1)} %refs_2_.1, bf16[1,4096,128]{2,1,0:T(8,128)(2,1)} %copy-done.7, bf16[1,4096,128]{2,1,0:T(8,128)(2,1)} %collective-permute-done.3.refs_4_, ...), custom_call_target="tpu_custom_call" | custom-call | flops 1207959552 | bytes 9437184 | tf_op jit(solution)/shard_map/pallas_call | solution.py:204
  177.5 6.6 %all-to-all-start.2 = ((bf16[24,8,4096]{2,1,0:T(8,128)(2,1)}), bf16[24,8,4096]{2,1,0:T(8,128)(2,1)S(1)}, u32[]{:S(2)}, u32[]{:S(2)}) async-start(bf16[24,8,4096]{2,1,0:T(8,128)(2,1)} %bitcast.28), calls=%async_computation.2 | async-start | bytes 3145728 | tf_op jit(solution)/shard_map/all_to_all | solution.py:366
  184.6 56.6 %all-to-all-done.2 = bf16[24,8,4096]{2,1,0:T(8,128)(2,1)S(1)} async-done(((bf16[24,8,4096]{2,1,0:T(8,128)(2,1)}), bf16[24,8,4096]{2,1,0:T(8,128)(2,1)S(1)}, u32[]{:S(2)}, u32[]{:S(2)}) %all-to-all-start.2) | async-done | bytes 1572896 | tf_op jit(solution)/shard_map/all_to_all | solution.py:366
  241.8 3.2 %collective-permute-start.5 = (bf16[32,4096]{1,0:T(8,128)(2,1)S(1)}, bf16[32,4096]{1,0:T(8,128)(2,1)S(1)}, u32[]{:S(2)}, u32[]{:S(2)}) collective-permute-start(bf16[32,4096]{1,0:T(8,128)(2,1)S(1)} %slice.42), channel_id=1, source_target_pairs={{0,1},{1,0},{2,3},{3,2},{4,5},{5,4},{6,7},{7,6},{8,9},{9,8},{10,11... | collective-permute-start | bytes 786440 | tf_op jit(solution)/shard_map/ppermute | solution.py:227
  245.0 1.1 collective-permute-done.5
  246.3 14.2 %all_to_all.21.terms_ref = bf16[8,4,4096]{2,1,0:T(4,128)(2,1)S(1)} all-to-all(bf16[8,4,4096]{2,1,0:T(4,128)(2,1)S(1)} %reshape.61), channel_id=1, replica_groups=mesh['z'=12,'xh'=2,'xl'=2,'y'=8,'core'=2] {'y'}, dimensions={0} | all-to-all | bytes 524288 | tf_op jit(solution)/shard_map/all_to_all | solution.py:233
  (49 shorter events, 5.3 us)
Async XLA Ops:
  0.0 69.9 %copy-start = (bf16[64,4096]{1,0:T(8,128)(2,1)S(1)}, bf16[64,4096]{1,0:T(8,128)(2,1)}, u32[]{:S(2)}) copy-start(bf16[64,4096]{1,0:T(8,128)(2,1)} %param.14) | copy-start | bytes 1572868
  0.0 58.3 %copy-start.5 = (bf16[1,4096,128]{2,1,0:T(8,128)(2,1)S(1)}, bf16[1,4096,128]{2,1,0:T(8,128)(2,1)}, u32[]{:S(2)}) copy-start(bf16[1,4096,128]{2,1,0:T(8,128)(2,1)} %refs_2_.1) | copy-start | bytes 3145732
  0.0 60.8 %copy-start.8 = (s32[64,8]{0,1:T(8,128)S(1)}, s32[64,8]{0,1:T(8,128)}, u32[]{:S(2)}) copy-start(s32[64,8]{0,1:T(8,128)} %param.24) | copy-start | bytes 6148
  0.0 60.9 %copy-start.9 = (s32[64,8]{0,1:T(8,128)S(1)}, s32[64,8]{0,1:T(8,128)}, u32[]{:S(2)}) copy-start(s32[64,8]{0,1:T(8,128)} %param.25) | copy-start | bytes 6148
  0.0 35.5 %collective-permute-start = (bf16[1,4096,128]{2,1,0:T(8,128)(2,1)}, bf16[1,4096,128]{2,1,0:T(8,128)(2,1)S(1)}, u32[]{:S(2)}, u32[]{:S(2)}) collective-permute-start(bf16[1,4096,128]{2,1,0:T(8,128)(2,1)} %refs_1_.1), channel_id=1, source_target_pairs={{0,16},{16,0},{1,17},{17,1},{2,18},{18,2},{3,19},{19,3},{4,20},{20... | collective-permute-start | bytes 3145736 | tf_op jit(solution)/shard_map/ppermute | solution.py:296
  4.7 56.6 %copy-start.3 = (s32[3]{0:T(128)S(1)}, s32[3]{0:T(128)}, u32[]{:S(2)}) copy-start(s32[3]{0:T(128)} %pad_add_fusion.place_ref.refs_0_) | copy-start | bytes 40
  35.5 1.0 copy-start.7
  47.2 14.0 %collective-permute-start.1 = (bf16[3072,128]{1,0:T(8,128)(2,1)S(1)}, bf16[3072,128]{1,0:T(8,128)(2,1)S(1)}, u32[]{:S(2)}, u32[]{:S(2)}) collective-permute-start(bf16[3072,128]{1,0:T(8,128)(2,1)S(1)} %bitcast.24), channel_id=1, source_target_pairs={{0,1},{1,0},{2,3},{3,2},{4,5},{5,4},{6,7},{7,6},{8,9},{9,8},{10,11... | collective-permute-start | bytes 2359304 | tf_op jit(solution)/shard_map/ppermute | solution.py:312
  58.3 48.7 %collective-permute-start.3 = (bf16[1,4096,128]{2,1,0:T(8,128)(2,1)S(1)}, bf16[1,4096,128]{2,1,0:T(8,128)(2,1)}, u32[]{:S(2)}, u32[]{:S(2)}) collective-permute-start(bf16[1,4096,128]{2,1,0:T(8,128)(2,1)S(1)} %copy-done.5), channel_id=1, source_target_pairs={{0,16},{16,0},{1,17},{17,1},{2,18},{18,2},{3,19},{19,3},{4,20},{20... | collective-permute-start | bytes 3145736 | tf_op jit(solution)/shard_map/ppermute | solution.py:297
  61.3 0.8 copy-start.1
  67.7 22.0 %copy-start.2 = (f32[4096]{0:T(1024)S(1)}, f32[4096]{0:T(1024)}, u32[]{:S(2)}) copy-start(f32[4096]{0:T(1024)} %param.20) | copy-start | bytes 49156
  67.7 3.4 %collective-permute-start.2 = (bf16[32,4096]{1,0:T(8,128)(2,1)S(1)}, bf16[32,4096]{1,0:T(8,128)(2,1)S(1)}, u32[]{:S(2)}, u32[]{:S(2)}) collective-permute-start(bf16[32,4096]{1,0:T(8,128)(2,1)S(1)} %slice.43), channel_id=1, source_target_pairs={{0,1},{1,0},{2,3},{3,2},{4,5},{5,4},{6,7},{7,6},{8,9},{9,8},{10,11... | collective-permute-start | bytes 786440 | tf_op jit(solution)/shard_map/ppermute | solution.py:227
  108.8 5.4 %copy-start.6 = (bf16[1,128,4096]{2,1,0:T(8,128)(2,1)S(1)}, bf16[1,128,4096]{2,1,0:T(8,128)(2,1)}, u32[]{:S(2)}) copy-start(bf16[1,128,4096]{2,1,0:T(8,128)(2,1)} %refs_5_.1) | copy-start | bytes 3145732
  108.8 62.6 %all-to-all-start.1 = ((bf16[24,8,4096]{2,1,0:T(8,128)(2,1)}), bf16[24,8,4096]{2,1,0:T(8,128)(2,1)S(1)}, u32[]{:S(2)}, u32[]{:S(2)}) async-start(bf16[24,8,4096]{2,1,0:T(8,128)(2,1)} %fusion), calls=%async_computation.1 | async-start | bytes 3145728 | tf_op jit(solution)/shard_map/all_to_all | solution.py:356
  114.2 33.9 %collective-permute-start.4 = (bf16[1,128,4096]{2,1,0:T(8,128)(2,1)S(1)}, bf16[1,128,4096]{2,1,0:T(8,128)(2,1)}, u32[]{:S(2)}, u32[]{:S(2)}) collective-permute-start(bf16[1,128,4096]{2,1,0:T(8,128)(2,1)S(1)} %copy-done.6), channel_id=1, source_target_pairs={{0,16},{16,0},{1,17},{17,1},{2,18},{18,2},{3,19},{19,3},{4,20},{20... | collective-permute-start | bytes 3145736 | tf_op jit(solution)/shard_map/ppermute | solution.py:298
  171.4 1.1 copy-start.4
  177.5 6.6 %copy-start.10 = (f32[64,8]{0,1:T(8,128)S(1)}, f32[64,8]{0,1:T(8,128)}, u32[]{:S(2)}) copy-start(f32[64,8]{0,1:T(8,128)} %param.26) | copy-start | bytes 6148
  177.5 63.7 %all-to-all-start.2 = ((bf16[24,8,4096]{2,1,0:T(8,128)(2,1)}), bf16[24,8,4096]{2,1,0:T(8,128)(2,1)S(1)}, u32[]{:S(2)}, u32[]{:S(2)}) async-start(bf16[24,8,4096]{2,1,0:T(8,128)(2,1)} %bitcast.28), calls=%async_computation.2 | async-start | bytes 3145728 | tf_op jit(solution)/shard_map/all_to_all | solution.py:366
  241.8 4.3 %collective-permute-start.5 = (bf16[32,4096]{1,0:T(8,128)(2,1)S(1)}, bf16[32,4096]{1,0:T(8,128)(2,1)S(1)}, u32[]{:S(2)}, u32[]{:S(2)}) collective-permute-start(bf16[32,4096]{1,0:T(8,128)(2,1)S(1)} %slice.42), channel_id=1, source_target_pairs={{0,1},{1,0},{2,3},{3,2},{4,5},{5,4},{6,7},{7,6},{8,9},{9,8},{10,11... | collective-permute-start | bytes 786440 | tf_op jit(solution)/shard_map/ppermute | solution.py:227

commit v5 on v4

--- a/solution.py
+++ b/solution.py
@@ -37,10 +37,12 @@
 
 
 def prepare_kernel(place_ref, kv_ref, q_ref, key_gain_ref, query_gain_ref, table_ref, mine_ref, query_ref):
-    rows, head_dim = mine_ref.shape
+    copies, rows, head_dim = mine_ref.shape
     table = table_ref[...]
     keys = norm_rotate(kv_ref[0].astype(jnp.float32), key_gain_ref[...], table)
-    mine_ref[...] = jnp.where(place_ref[0] == 0, keys.astype(jnp.bfloat16), kv_ref[1])
+    mine = jnp.where(place_ref[0] == 0, keys.astype(jnp.bfloat16), kv_ref[1])
+    for i in range(copies):
+        mine_ref[i] = mine
     for h in range(q_ref.shape[1] // head_dim):
         head = q_ref[:, h * head_dim : (h + 1) * head_dim].astype(jnp.float32)
         query_ref[h * rows : (h + 1) * rows, :] = norm_rotate(
@@ -48,7 +50,7 @@
         ).astype(jnp.bfloat16)
 
 
-def prepare(place, key_value, queries, key_gain, query_gain, table):
+def prepare(place, key_value, queries, key_gain, query_gain, table, copies):
     rows, width = queries.shape
     head_dim = table.shape[1]
     fixed = lambda i, place: (0, 0)
@@ -65,12 +67,12 @@
                 pl.BlockSpec((rows, head_dim), lambda i, place: (place[1], 0)),
             ],
             out_specs=[
-                pl.BlockSpec((rows, head_dim), fixed),
+                pl.BlockSpec((copies, rows, head_dim), lambda i, place: (0, 0, 0)),
                 pl.BlockSpec((rows * width // head_dim, head_dim), fixed),
             ],
         ),
         out_shape=[
-            jax.ShapeDtypeStruct((rows, head_dim), jnp.bfloat16),
+            jax.ShapeDtypeStruct((copies, rows, head_dim), jnp.bfloat16),
             jax.ShapeDtypeStruct((rows * width // head_dim, head_dim), jnp.bfloat16),
         ],
         compiler_params=pltpu.CompilerParams(vmem_limit_bytes=59 * 1024 * 1024),
@@ -145,6 +147,37 @@
     )(place, query, mine, other)
 
 
+def project_kernel(attended_ref, weight_ref, give_ref, keep_ref):
+    attended = attended_ref[...]
+    half = attended.shape[0] // 2
+    columns = 1024
+    for j in range(weight_ref.shape[1] // columns):
+        part = pl.ds(j * columns, columns)
+        product = jnp.dot(attended, weight_ref[:, part], preferred_element_type=jnp.float32)
+        give_ref[:, part] = product[:half].astype(jnp.bfloat16)
+        keep_ref[:, part] = product[half:]
+
+
+def project(attended, weight):
+    shape = (attended.shape[0] // 2, weight.shape[1])
+    whole = pl.BlockSpec(memory_space=pltpu.VMEM)
+    return pl.pallas_call(
+        project_kernel,
+        in_specs=[whole] * 2,
+        out_specs=[whole] * 2,
+        out_shape=[
+            jax.ShapeDtypeStruct(shape, jnp.bfloat16),
+            jax.ShapeDtypeStruct(shape, jnp.float32),
+        ],
+        compiler_params=pltpu.CompilerParams(vmem_limit_bytes=12 * 1024 * 1024),
+        cost_estimate=pl.CostEstimate(
+            flops=2 * attended.shape[0] * weight.shape[0] * weight.shape[1],
+            bytes_accessed=2 * weight.shape[0] * weight.shape[1],
+            transcendentals=0,
+        ),
+    )(attended, weight)
+
+
 def expert_kernel(chunks, *refs):
     x_ref, ga_ref, ua_ref, gb_ref, ub_ref, da_ref, db_ref, out_ref, x, into, back, out, sems = refs
     width = x.shape[1]
@@ -304,15 +337,15 @@
         key_norm_gain[None, :],
         query_gain[None, :],
         table,
-    )
-    mine = lax.all_gather(mine[None], "z", axis=0, tiled=True)
+        n_z,
+    )
+    mine = lax.all_to_all(mine, "z", split_axis=0, concat_axis=0, tiled=True)
     mine, gate_other = lax.optimization_barrier((mine, gate_other))
     mine = lax.all_gather(mine[None], ("xh", "xl"), axis=0, tiled=True)
     mine = mine.reshape(n_ctx * rows, head_dim)
     other = lax.ppermute(mine, "core", SWAP)
     attended = attend(place, query, mine, other, rows, n_x)
-    product = jnp.dot(attended, output_weight, preferred_element_type=jnp.float32)
-    give, keep = product[: rows // 2], product[rows // 2 :]
+    give, keep = project(attended, output_weight)
     local = EXPERTS // n_exp
     pairs = SLICES // 2
     peers = local * pairs

time: 262 us -> 260 us (level)
  matrix products: 5.22 us -> 2.19 us
    all_gather x1 -> x0, blocking collectives: 28 us -> none  [body(): mine = lax.all_gather(mine[None], 'z', axis=0, tiled=True)]
    all_to_all x0 -> x1, blocking collectives: none -> 27.1 us  [body(): mine = lax.all_to_all(mine, 'z', split_axis=0, concat_axis=0, tiled=True)]
    all_to_all x1, starting transfers between devices: 5.41 us -> 9.92 us  [body(): lax.all_to_all(outgoing, ('z', 'xh'), split_axis=0, concat_axis=0, tiled=...]
    dot_general x1 -> x0, matrix products: 3.03 us -> none  [body(): jnp.dot(attended, output_weight, preferred_element_type=jnp.float32)]
    ppermute x1, starting transfers between devices: 11.1 us -> 8.35 us  [body(): other = lax.ppermute(mine, 'core', SWAP)]
  transfers between devices with their start and end apart: 8 -> 8, of which waited for: 5 -> 5; matrix products, arithmetic and copies ran while one was open for 2% -> 1% of each run, Pallas kernels for 2% -> 2%
where the time goes in v5:
time: 260 us; the launch traced here: 259 us
  waiting for transfers between devices  114 us (44%)
  blocking collectives  87.2 us (34%)
  starting transfers between devices  37.9 us (15%)
  Pallas kernels  11.8 us (5%)
  local copies, waits for them, and re-layouts  4.09 us (2%)
    all_to_all x1, waiting for transfers between devices, body(): lax.all_to_all(pieces, ('z', 'xh'), split_axis=0, concat_axis=0, tiled=True)  56.6 us
    all_to_all x2, blocking collectives, to_owners(): return lax.all_to_all(blocks, 'y', split_axis=0, concat_axis=0, tiled=True)  33.1 us
    ppermute x1, waiting for transfers between devices, body(): down_other = lax.ppermute(down_weight, 'xl', SWAP)  32.1 us
    all_to_all x1, blocking collectives, body(): mine = lax.all_to_all(mine, 'z', split_axis=0, concat_axis=0, tiled=True)  27.1 us
    all_to_all x1, waiting for transfers between devices, body(): lax.all_to_all(outgoing, ('z', 'xh'), split_axis=0, concat_axis=0, tiled=...  23.1 us
    all_gather x1, blocking collectives, body(): normed = lax.all_gather(own_normed, EXP, axis=0, tiled=True)  16.5 us
    all_gather x1, blocking collectives, body(): mine = lax.all_gather(mine[None], ('xh', 'xl'), axis=0, tiled=True)  10.5 us
    all_to_all x1, starting transfers between devices, body(): lax.all_to_all(outgoing, ('z', 'xh'), split_axis=0, concat_axis=0, tiled=...  9.92 us
  transfers between devices with their start and end apart: 8, of which 5 were waited for; matrix products, arithmetic and copies ran while one was open for 1% of the time, Pallas kernels for 2%

profile of v5, /device:TPU:1, one launch (start us, length us, event | category | flops | bytes accessed | tf_op | source)
XLA Modules:
  0.0 259.5 jit_solution(10452976608292701966)
XLA Ops:
  0.0 4.1 %collective-permute-start = (bf16[1,4096,128]{2,1,0:T(8,128)(2,1)}, bf16[1,4096,128]{2,1,0:T(8,128)(2,1)}, u32[]{:S(2)}, u32[]{:S(2)}) collective-permute-start(bf16[1,4096,128]{2,1,0:T(8,128)(2,1)} %refs_1_.1), channel_id=1, source_target_pairs={{0,16},{16,0},{1,17},{17,1},{2,18},{18,2},{3,19},{19,3},{4,20},{20... | collective-permute-start | bytes 3145736 | tf_op jit(solution)/shard_map/ppermute | solution.py:329
  4.8 2.7 %shard_map.136 = (bf16[12,64,128]{2,1,0:T(8,128)(2,1)}, bf16[256,128]{1,0:T(8,128)(2,1)}) custom-call(s32[3]{0:T(128)} %pad_add_fusion.place_ref.refs_0_, bf16[2,64,512]{2,1,0:T(8,128)(2,1)} %kv_ref.1, bf16[64,512]{1,0:T(8,128)(2,1)} %q_ref.1, f32[1,128]{1,0:T(1,128)} %bitcast.27, f32[1,128]{1,0:T(1,128)} %bitcast.28, f32[3072,128]{1,0:T(8,128)} %constant.81.clone.table_ref), custom_call_target="tpu_custom_call" | custom-call | tf_op jit(solution)/shard_map/pallas_call | solution.py:57
  7.5 27.1 %all_to_all.25 = bf16[12,64,128]{2,1,0:T(8,128)(2,1)S(1)} all-to-all(bf16[12,64,128]{2,1,0:T(8,128)(2,1)} %get-tuple-element.19), channel_id=1, replica_groups=mesh['z'=12,'xh'=2,'xl'=2,'y'=8,'core'=2] {'z'}, dimensions={0} | all-to-all | bytes 393216 | tf_op jit(solution)/shard_map/all_to_all | solution.py:342
  34.6 10.5 %all-gather = bf16[48,64,128]{2,1,0:T(8,128)(2,1)S(1)} all-gather(bf16[12,64,128]{2,1,0:T(8,128)(2,1)S(1)} %all_to_all.25), channel_id=2, replica_groups=mesh['z'=12,'xh'=2,'xl'=2,'y'=8,'core'=2] {'xh','xl'}, dimensions={0}, use_global_device_ids=true | all-gather | bytes 983040 | tf_op jit(solution)/shard_map/all_gather | solution.py:344
  45.1 8.3 %collective-permute-start.1 = (bf16[3072,128]{1,0:T(8,128)(2,1)S(1)}, bf16[3072,128]{1,0:T(8,128)(2,1)S(1)}, u32[]{:S(2)}, u32[]{:S(2)}) collective-permute-start(bf16[3072,128]{1,0:T(8,128)(2,1)S(1)} %bitcast.21), channel_id=1, source_target_pairs={{0,1},{1,0},{2,3},{3,2},{4,5},{5,4},{6,7},{7,6},{8,9},{9,8},{10,11... | collective-permute-start | bytes 2359304 | tf_op jit(solution)/shard_map/ppermute | solution.py:346
  53.4 1.9 collective-permute-start.3
  55.9 2.5 shard_map.137.attended_ref
  58.4 2.2 copy-done.1
  61.4 2.0 collective-permute-start.2
  63.5 1.4 collective-permute-done.2
  65.0 18.9 %all_to_all.26.terms_ref = bf16[8,4,4096]{2,1,0:T(4,128)(2,1)S(1)} all-to-all(bf16[8,4,4096]{2,1,0:T(4,128)(2,1)S(1)} %reshape.56), channel_id=1, replica_groups=mesh['z'=12,'xh'=2,'xl'=2,'y'=8,'core'=2] {'y'}, dimensions={0} | all-to-all | bytes 524288 | tf_op jit(solution)/shard_map/all_to_all | solution.py:266
  84.1 16.5 %all-gather.1 = bf16[16,4,4096]{2,1,0:T(4,128)(2,1)S(1)} all-gather(bf16[1,4,4096]{2,1,0:T(4,128)(2,1)S(1)} %bitcast.23), channel_id=1, replica_groups=mesh['z'=12,'xh'=2,'xl'=2,'y'=8,'core'=2] {'y','core'}, dimensions={0}, use_global_device_ids=true | all-gather | bytes 557056 | tf_op jit(solution)/shard_map/all_gather | solution.py:373
  100.8 1.8 fusion
  102.5 9.9 %all-to-all-start.2 = ((bf16[24,8,4096]{2,1,0:T(8,128)(2,1)}), bf16[24,8,4096]{2,1,0:T(8,128)(2,1)S(1)}, u32[]{:S(2)}, u32[]{:S(2)}) async-start(bf16[24,8,4096]{2,1,0:T(8,128)(2,1)} %fusion), calls=%async_computation.2 | async-start | bytes 3145728 | tf_op jit(solution)/shard_map/all_to_all | solution.py:389
  112.5 1.9 collective-permute-start.4
  114.4 32.1 %collective-permute-done.4.refs_6_ = bf16[1,128,4096]{2,1,0:T(8,128)(2,1)} collective-permute-done((bf16[1,128,4096]{2,1,0:T(8,128)(2,1)S(1)}, bf16[1,128,4096]{2,1,0:T(8,128)(2,1)}, u32[]{:S(2)}, u32[]{:S(2)}) %collective-permute-start.4) | collective-permute-done | bytes 1048608 | tf_op jit(solution)/shard_map/ppermute | solution.py:331
  146.5 23.1 %all-to-all-done.2 = bf16[24,8,4096]{2,1,0:T(8,128)(2,1)S(1)} async-done(((bf16[24,8,4096]{2,1,0:T(8,128)(2,1)}), bf16[24,8,4096]{2,1,0:T(8,128)(2,1)S(1)}, u32[]{:S(2)}, u32[]{:S(2)}) %all-to-all-start.2) | async-done | bytes 1572896 | tf_op jit(solution)/shard_map/all_to_all | solution.py:389
  169.7 1.2 copy-done.5
  170.8 5.0 %shard_map.140 = bf16[192,4096]{1,0:T(8,128)(2,1)} custom-call(bf16[192,4096]{1,0:T(8,128)(2,1)} %bitcast.26, bf16[1,4096,128]{2,1,0:T(8,128)(2,1)} %refs_1_.1, bf16[1,4096,128]{2,1,0:T(8,128)(2,1)} %refs_2_.1, bf16[1,4096,128]{2,1,0:T(8,128)(2,1)} %collective-permute-done.refs_3_, bf16[1,4096,128]{2,1,0:T(8,128)(2,1)} %collective-permute-done.3.refs_4_, ...), custom_call_target="tpu_custom_call" | custom-call | flops 1207959552 | bytes 9437184 | tf_op jit(solution)/shard_map/pallas_call | solution.py:237
  175.8 6.6 %all-to-all-start.3 = ((bf16[24,8,4096]{2,1,0:T(8,128)(2,1)}), bf16[24,8,4096]{2,1,0:T(8,128)(2,1)S(1)}, u32[]{:S(2)}, u32[]{:S(2)}) async-start(bf16[24,8,4096]{2,1,0:T(8,128)(2,1)} %bitcast.25), calls=%async_computation.3 | async-start | bytes 3145728 | tf_op jit(solution)/shard_map/all_to_all | solution.py:399
  182.9 56.6 %all-to-all-done.3 = bf16[24,8,4096]{2,1,0:T(8,128)(2,1)S(1)} async-done(((bf16[24,8,4096]{2,1,0:T(8,128)(2,1)}), bf16[24,8,4096]{2,1,0:T(8,128)(2,1)S(1)}, u32[]{:S(2)}, u32[]{:S(2)}) %all-to-all-start.3) | async-done | bytes 1572896 | tf_op jit(solution)/shard_map/all_to_all | solution.py:399
  240.1 3.2 %collective-permute-start.5 = (bf16[32,4096]{1,0:T(8,128)(2,1)S(1)}, bf16[32,4096]{1,0:T(8,128)(2,1)S(1)}, u32[]{:S(2)}, u32[]{:S(2)}) collective-permute-start(bf16[32,4096]{1,0:T(8,128)(2,1)S(1)} %slice.27), channel_id=1, source_target_pairs={{0,1},{1,0},{2,3},{3,2},{4,5},{5,4},{6,7},{7,6},{8,9},{9,8},{10,11... | collective-permute-start | bytes 786440 | tf_op jit(solution)/shard_map/ppermute | solution.py:260
  243.2 1.1 collective-permute-done.5
  244.5 14.3 %all_to_all.27.terms_ref = bf16[8,4,4096]{2,1,0:T(4,128)(2,1)S(1)} all-to-all(bf16[8,4,4096]{2,1,0:T(4,128)(2,1)S(1)} %reshape.61), channel_id=1, replica_groups=mesh['z'=12,'xh'=2,'xl'=2,'y'=8,'core'=2] {'y'}, dimensions={0} | all-to-all | bytes 524288 | tf_op jit(solution)/shard_map/all_to_all | solution.py:266
  (48 shorter events, 4.3 us)
Async XLA Ops:
  0.0 63.4 %copy-start = (bf16[64,4096]{1,0:T(8,128)(2,1)S(1)}, bf16[64,4096]{1,0:T(8,128)(2,1)}, u32[]{:S(2)}) copy-start(bf16[64,4096]{1,0:T(8,128)(2,1)} %param.14) | copy-start | bytes 1572868
  0.0 34.6 %collective-permute-start = (bf16[1,4096,128]{2,1,0:T(8,128)(2,1)}, bf16[1,4096,128]{2,1,0:T(8,128)(2,1)}, u32[]{:S(2)}, u32[]{:S(2)}) collective-permute-start(bf16[1,4096,128]{2,1,0:T(8,128)(2,1)} %refs_1_.1), channel_id=1, source_target_pairs={{0,16},{16,0},{1,17},{17,1},{2,18},{18,2},{3,19},{19,3},{4,20},{20... | collective-permute-start | bytes 3145736 | tf_op jit(solution)/shard_map/ppermute | solution.py:329
  4.8 48.7 %copy-start.6 = (bf16[1,4096,128]{2,1,0:T(8,128)(2,1)S(1)}, bf16[1,4096,128]{2,1,0:T(8,128)(2,1)}, u32[]{:S(2)}) copy-start(bf16[1,4096,128]{2,1,0:T(8,128)(2,1)} %refs_2_.1) | copy-start | bytes 3145732
  4.8 50.6 %copy-start.8 = (s32[64,8]{0,1:T(8,128)S(1)}, s32[64,8]{0,1:T(8,128)}, u32[]{:S(2)}) copy-start(s32[64,8]{0,1:T(8,128)} %param.24) | copy-start | bytes 6148
  4.8 50.7 %copy-start.9 = (s32[64,8]{0,1:T(8,128)S(1)}, s32[64,8]{0,1:T(8,128)}, u32[]{:S(2)}) copy-start(s32[64,8]{0,1:T(8,128)} %param.25) | copy-start | bytes 6148
  4.8 51.1 %copy-start.4 = (s32[3]{0:T(128)S(1)}, s32[3]{0:T(128)}, u32[]{:S(2)}) copy-start(s32[3]{0:T(128)} %pad_add_fusion.place_ref.refs_0_) | copy-start | bytes 40
  7.5 48.4 %copy-start.2 = (bf16[256,128]{1,0:T(8,128)(2,1)S(1)}, bf16[256,128]{1,0:T(8,128)(2,1)}, u32[]{:S(2)}) copy-start(bf16[256,128]{1,0:T(8,128)(2,1)} %get-tuple-element.18.refs_1_) | copy-start | bytes 196612
  45.1 10.8 %collective-permute-start.1 = (bf16[3072,128]{1,0:T(8,128)(2,1)S(1)}, bf16[3072,128]{1,0:T(8,128)(2,1)S(1)}, u32[]{:S(2)}, u32[]{:S(2)}) collective-permute-start(bf16[3072,128]{1,0:T(8,128)(2,1)S(1)} %bitcast.21), channel_id=1, source_target_pairs={{0,1},{1,0},{2,3},{3,2},{4,5},{5,4},{6,7},{7,6},{8,9},{9,8},{10,11... | collective-permute-start | bytes 2359304 | tf_op jit(solution)/shard_map/ppermute | solution.py:346
  53.4 47.3 %collective-permute-start.3 = (bf16[1,4096,128]{2,1,0:T(8,128)(2,1)S(1)}, bf16[1,4096,128]{2,1,0:T(8,128)(2,1)}, u32[]{:S(2)}, u32[]{:S(2)}) collective-permute-start(bf16[1,4096,128]{2,1,0:T(8,128)(2,1)S(1)} %copy-done.6), channel_id=1, source_target_pairs={{0,16},{16,0},{1,17},{17,1},{2,18},{18,2},{3,19},{19,3},{4,20},{20... | collective-permute-start | bytes 3145736 | tf_op jit(solution)/shard_map/ppermute | solution.py:330
  58.4 2.2 copy-start.1
  61.4 22.5 %copy-start.3 = (f32[4096]{0:T(1024)S(1)}, f32[4096]{0:T(1024)}, u32[]{:S(2)}) copy-start(f32[4096]{0:T(1024)} %param.20) | copy-start | bytes 49156
  61.4 3.4 %collective-permute-start.2 = (bf16[32,4096]{1,0:T(8,128)(2,1)S(1)}, bf16[32,4096]{1,0:T(8,128)(2,1)S(1)}, u32[]{:S(2)}, u32[]{:S(2)}) collective-permute-start(bf16[32,4096]{1,0:T(8,128)(2,1)S(1)} %get-tuple-element.22), channel_id=1, source_target_pairs={{0,1},{1,0},{2,3},{3,2},{4,5},{5,4},{6,7},{7,6},{8,9},{9,8},{10,11... | collective-permute-start | bytes 786440 | tf_op jit(solution)/shard_map/ppermute | solution.py:260
  102.5 9.9 %copy-start.7 = (bf16[1,128,4096]{2,1,0:T(8,128)(2,1)S(1)}, bf16[1,128,4096]{2,1,0:T(8,128)(2,1)}, u32[]{:S(2)}) copy-start(bf16[1,128,4096]{2,1,0:T(8,128)(2,1)} %refs_5_.1) | copy-start | bytes 3145732
  102.5 67.1 %all-to-all-start.2 = ((bf16[24,8,4096]{2,1,0:T(8,128)(2,1)}), bf16[24,8,4096]{2,1,0:T(8,128)(2,1)S(1)}, u32[]{:S(2)}, u32[]{:S(2)}) async-start(bf16[24,8,4096]{2,1,0:T(8,128)(2,1)} %fusion), calls=%async_computation.2 | async-start | bytes 3145728 | tf_op jit(solution)/shard_map/all_to_all | solution.py:389
  112.5 34.0 %collective-permute-start.4 = (bf16[1,128,4096]{2,1,0:T(8,128)(2,1)S(1)}, bf16[1,128,4096]{2,1,0:T(8,128)(2,1)}, u32[]{:S(2)}, u32[]{:S(2)}) collective-permute-start(bf16[1,128,4096]{2,1,0:T(8,128)(2,1)S(1)} %copy-done.7), channel_id=1, source_target_pairs={{0,16},{16,0},{1,17},{17,1},{2,18},{18,2},{3,19},{19,3},{4,20},{20... | collective-permute-start | bytes 3145736 | tf_op jit(solution)/shard_map/ppermute | solution.py:331
  169.7 1.2 copy-start.5
  175.8 6.6 %copy-start.10 = (f32[64,8]{0,1:T(8,128)S(1)}, f32[64,8]{0,1:T(8,128)}, u32[]{:S(2)}) copy-start(f32[64,8]{0,1:T(8,128)} %param.26) | copy-start | bytes 6148
  175.8 63.7 %all-to-all-start.3 = ((bf16[24,8,4096]{2,1,0:T(8,128)(2,1)}), bf16[24,8,4096]{2,1,0:T(8,128)(2,1)S(1)}, u32[]{:S(2)}, u32[]{:S(2)}) async-start(bf16[24,8,4096]{2,1,0:T(8,128)(2,1)} %bitcast.25), calls=%async_computation.3 | async-start | bytes 3145728 | tf_op jit(solution)/shard_map/all_to_all | solution.py:399
  240.1 4.3 %collective-permute-start.5 = (bf16[32,4096]{1,0:T(8,128)(2,1)S(1)}, bf16[32,4096]{1,0:T(8,128)(2,1)S(1)}, u32[]{:S(2)}, u32[]{:S(2)}) collective-permute-start(bf16[32,4096]{1,0:T(8,128)(2,1)S(1)} %slice.27), channel_id=1, source_target_pairs={{0,1},{1,0},{2,3},{3,2},{4,5},{5,4},{6,7},{7,6},{8,9},{9,8},{10,11... | collective-permute-start | bytes 786440 | tf_op jit(solution)/shard_map/ppermute | solution.py:260
